TPU v7x, 32 devices: a whole 2x2x4 slice. The times are simulated.
32 devices in a mesh: dp: 4 (over z), row: 4 (over y, x), col: 2 (over core).
Axes of the slice: x: 2, y: 2, z: 4, core: 2. Of those that a mesh axis runs over, the one named last changes fastest.
Arguments:
- tokens: bfloat16 [9232, 1024], P('dp', ('row', 'col')), may hold values from -80 to 80
- projector: bfloat16 [3, 1024, 1024], P(None, 'row', 'col'), may hold values from -0.25 to 0.25
- offsets: float32 [2, 1024], P(None, 'col'), may hold values from -3 to 3
- combiner: bfloat16 [1024, 1024], P('col', 'row'), may hold values from -0.25 to 0.25
- baseline: float32 [1024], P(('row', 'col')), may hold values from -2 to 2
- widener: bfloat16 [1024, 4096], P('row', 'col'), may hold values from -0.1875 to 0.1875
- thresholds: float32 [4096], P('col'), may hold values from -3 to 3
- narrower: bfloat16 [4096, 1024], P('col', 'row'), may hold values from -0.125 to 0.125
- residue: float32 [1024], P(('row', 'col')), may hold values from -2 to 2
- stretch: float32 [1024], P(('row', 'col')), may hold values from 0.5 to 1.5
- lifting: float32 [1024], P(('row', 'col')), may hold values from -2 to 2
- dilation: float32 [1024], P(('row', 'col')), may hold values from 0.5 to 1.5
- elevation: float32 [1024], P(('row', 'col')), may hold values from -2 to 2
- cotangent: bfloat16 [9232, 1024], P('dp', ('row', 'col')), may hold values from -6 to 6
Outputs:
- layer_output: float32 [9232, 1024], P('dp', ('row', 'col'))
- tokens_delta: float32 [9232, 1024], P('dp', ('row', 'col'))
- projector_delta: float32 [3, 1024, 1024], P(None, 'row', 'col')
- offsets_delta: float32 [2, 1024], P(None, 'col')
- combiner_delta: float32 [1024, 1024], P('col', 'row')
- baseline_delta: float32 [1024], P(('row', 'col'))
- widener_delta: float32 [1024, 4096], P('row', 'col')
- thresholds_delta: float32 [4096], P('col')
- narrower_delta: float32 [4096, 1024], P('col', 'row')
- residue_delta: float32 [1024], P(('row', 'col'))
- stretch_delta: float32 [1024], P(('row', 'col'))
- lifting_delta: float32 [1024], P(('row', 'col'))
- dilation_delta: float32 [1024], P(('row', 'col'))
- elevation_delta: float32 [1024], P(('row', 'col'))
All inputs are finite; a program needn't handle non-finite values.
Results may differ from a plain program's by a relative error of at most 0.015.
Values may be sent and summed in bfloat16 or wider, within the bound.
No kernel may reach another device: no remote copies, remote signals or barrier semaphores. Data moves between devices by JAX's collectives and lax.ppermute only.
A program may use at most 128 MiB of HBM per device.

v0:
```python
import jax
import jax.numpy as jnp
from jax import lax
from jax.experimental import pallas as pl
from jax.experimental.pallas import tpu as pltpu
from jax.sharding import PartitionSpec as P

D = 1024
HD = 64
SEQ = 577
PAD = 592
RB = 4
KB = D // RB
PLANE = 96
SHARED = 80
TOP = 304

NORM_EPSILON = 1e-05
SIGMOID_SLOPE = 1.702
F32 = jnp.float32
BF16 = jnp.bfloat16
VMEM_LIMIT = 60 * 1024 * 1024
SHRINK = 64
DEPTH = 2

STRETCH, LIFTING, BASELINE, DILATION, ELEVATION, RESIDUE = range(6)


def mm(a, b):
    return lax.dot_general(a, b, (((1,), (0,)), ((), ())), preferred_element_type=F32)


def mm_nt(a, b):
    return lax.dot_general(a, b, (((1,), (1,)), ((), ())), preferred_element_type=F32)


def mm_tn(a, b):
    return lax.dot_general(a, b, (((0,), (0,)), ((), ())), preferred_element_type=F32)


def sds(shape, dtype=BF16):
    return jax.ShapeDtypeStruct(shape, dtype)


def whole(shape):
    return pl.BlockSpec(shape, lambda *_: (0,) * len(shape))


def call(body, grid, in_specs, out_specs, out_shape, flops, nbytes, scratch=(), transcendentals=0):
    return pl.pallas_call(
        body,
        grid=grid,
        in_specs=in_specs,
        out_specs=out_specs,
        out_shape=out_shape,
        scratch_shapes=list(scratch),
        compiler_params=pltpu.CompilerParams(
            vmem_limit_bytes=VMEM_LIMIT, dimension_semantics=("arbitrary",) * len(grid)
        ),
        cost_estimate=pl.CostEstimate(
            flops=int(flops) // SHRINK, bytes_accessed=int(nbytes) // SHRINK, transcendentals=int(transcendentals) // SHRINK
        ),
    )


PIECES = (TOP, PAD - TOP)


def piece_specs():
    return [pl.BlockSpec((rows, D), lambda *step: (0, 0)) for rows in PIECES]


def piece_shapes():
    return [sds((rows, D)) for rows in PIECES]


def store_pieces(refs, value):
    refs[0][...] = value[:TOP].astype(BF16)
    refs[1][...] = value[TOP:].astype(BF16)


def load_sum(pieces):
    top, bottom, other_top, other_bottom = [piece[...].astype(F32) for piece in pieces]
    return jnp.concatenate([top + other_top, bottom + other_bottom], axis=0)


def row_mask(shape):
    return lax.broadcasted_iota(jnp.int32, shape, 0) < SEQ


def standardize(value):
    average = jnp.mean(value, axis=1, keepdims=True)
    centred = value - average
    spread = jnp.mean(centred * centred, axis=1, keepdims=True)
    reciprocal = lax.rsqrt(spread + NORM_EPSILON)
    return centred * reciprocal, reciprocal


def norm_backward(upstream, standard, reciprocal, gain):
    scaled = upstream * gain
    mean_scaled = jnp.mean(scaled, axis=1, keepdims=True)
    mean_along = jnp.mean(scaled * standard, axis=1, keepdims=True)
    return reciprocal * (scaled - mean_scaled - standard * mean_along)


def norm_kernel(x, vec, cot, normed, normed_t, cot_t):
    standard, _r = standardize(x[...].astype(F32))
    value = standard * vec[STRETCH : STRETCH + 1] + vec[LIFTING : LIFTING + 1]
    normed[...] = value.astype(BF16)
    normed_t[...] = value.T.astype(BF16)
    cot_t[...] = cot[...].astype(F32).T.astype(BF16)


def norm_call(x, vec, cot):
    return call(
        norm_kernel,
        (1,),
        [whole((PAD, D)), whole(vec.shape), whole((PAD, D))],
        [whole((PAD, D)), whole((D, PAD)), whole((D, PAD))],
        [sds((PAD, D)), sds((D, PAD)), sds((D, PAD))],
        10 * PAD * D,
        10 * PAD * D,
    )(x, vec, cot)


BLOCK_ROWS = (KB, PLANE + SHARED, PLANE + SHARED, PLANE, SHARED, SHARED, SHARED, SHARED)


def weight_specs(tile, at):
    pieces = [pl.BlockSpec((rows, tile), lambda *step: (0, at(*step))) for rows in BLOCK_ROWS]
    return [pl.BlockSpec(memory_space=pltpu.SMEM)] + pieces


def plain_specs(tile, at):
    half = pl.BlockSpec((KB // 2, tile), lambda *step: (0, at(*step)))
    return [pl.BlockSpec((KB, tile), lambda *step: (0, at(*step)))] * 3 + [half] * 2


def weight_buffer(tile):
    return pltpu.VMEM((RB, KB, tile), BF16)


def joined(pieces, buffer):
    plane, own, near_x, near_y, far_plane, far_shared, other_x, other_y, other_far = pieces
    mine = pl.multiple_of(PLANE + SHARED * plane[0], 16)
    others = pl.multiple_of(PLANE + SHARED * (1 - plane[0]), 16)
    buffer[0] = own[...]
    for k, (near, other) in enumerate(((near_x, other_x), (near_y, other_y)), 1):
        buffer[k, :PLANE] = near[:PLANE]
        buffer[k, pl.ds(mine, SHARED)] = near[PLANE:]
        buffer[k, pl.ds(others, SHARED)] = other[...]
    buffer[3, :PLANE] = far_plane[...]
    buffer[3, pl.ds(mine, SHARED)] = far_shared[...]
    buffer[3, pl.ds(others, SHARED)] = other_far[...]
    return buffer[...].reshape(D, buffer.shape[2])


def qkv_kernel(normed, *rest):
    weights, (bias, qkv, buffer) = rest[:9], rest[9:]
    qkv[...] = (bias[0] + mm(normed[...], joined(weights, buffer))).astype(BF16)


def qkv_call(normed, blocks, bias):
    width = bias.shape[2]
    return call(
        qkv_kernel,
        (3,),
        [whole((PAD, D))]
        + weight_specs(width, lambda j: j)
        + [pl.BlockSpec((1, 1, width), lambda j: (j, 0, 0))],
        pl.BlockSpec((PAD, width), lambda j: (0, j)),
        sds((PAD, 3 * width)),
        2 * PAD * D * 3 * width,
        2 * D * 3 * width + 2 * PAD * D + 6 * PAD * width,
        [weight_buffer(width)],
    )(normed, *blocks, bias)


def head_mask(i, shape):
    lane = lax.broadcasted_iota(jnp.int32, shape, 1)
    return (lane >= i * HD) & (lane < (i + 1) * HD)


def attend_kernel(q, k, v, mixed, probs):
    queries = q[...]
    keys = k[...]
    values_t = v[...].astype(F32).T.astype(BF16)
    outs = []
    for i in range(2):
        picked = jnp.where(head_mask(i, queries.shape), queries.astype(F32) * HD ** (-0.5), 0.0)
        scores = mm_nt(keys, picked.astype(BF16))
        scores = jnp.where(row_mask(scores.shape), scores, -1e30)
        top = jnp.max(scores, axis=0, keepdims=True)
        weights = jnp.exp(scores - top)
        total = jnp.sum(weights, axis=0, keepdims=True)
        rounded = (weights * (1.0 / total)).astype(BF16)
        probs[i] = rounded
        outs.append(mm(values_t[i * HD : (i + 1) * HD], rounded))
    mixed[...] = jnp.concatenate(outs, axis=0).T.astype(BF16)


def attend_call(qkv):
    width = qkv.shape[1] // 3
    pairs = width // 128
    spec = lambda j: pl.BlockSpec((PAD, 128), lambda h, j=j: (0, j * pairs + h))
    return call(
        attend_kernel,
        (pairs,),
        [spec(0), spec(1), spec(2)],
        [pl.BlockSpec((PAD, 128), lambda h: (0, h)), pl.BlockSpec((2, PAD, PAD), lambda h: (h, 0, 0))],
        [sds((PAD, width)), sds((2 * pairs, PAD, PAD))],
        pairs * 2 * 2 * 2 * PAD * PAD * 128,
        pairs * 2 * PAD * PAD * 2,
        transcendentals=pairs * 2 * PAD * PAD,
    )(qkv, qkv, qkv)


def combine_kernel(mixed, *rest):
    top, bottom, buffer = rest[9:]
    store_pieces((top, bottom), mm_nt(mixed[...], joined(rest[:9], buffer)))


def combine_call(mixed, blocks):
    width = mixed.shape[1]
    return call(
        combine_kernel,
        (1,),
        [whole((PAD, width))] + weight_specs(width, lambda i: 3),
        piece_specs(),
        piece_shapes(),
        2 * PAD * D * width,
        2 * (PAD * D + width * D + PAD * width),
        [weight_buffer(width)],
    )(mixed, *blocks)


def split_rows(value, refs):
    own, first_x, first_y, later_x, later_y = refs
    half = KB // 2
    value = value.astype(BF16)
    own[...] = value[:KB]
    first_x[:half] = value[6 * half : 7 * half]
    first_x[half:] = value[2 * half : 3 * half]
    first_y[:half] = value[7 * half :]
    first_y[half:] = value[5 * half : 6 * half]
    later_x[...] = value[3 * half : 4 * half]
    later_y[...] = value[4 * half : 5 * half]


def delta_specs(tile, at):
    half = KB // 2
    return [pl.BlockSpec((KB, tile), at)] * 3 + [pl.BlockSpec((half, tile), at)] * 2


def delta_shapes(width):
    half = KB // 2
    return [sds((KB, width))] * 3 + [sds((half, width))] * 2


def forward_kernel(x, *rest):
    parts, vec, rest = rest[:4], rest[4], rest[5:]
    weights, (thresholds, cot_t), rest = rest[:9], rest[9:11], rest[11:]
    resid, normed_t, hidden, slope = rest[:4]
    deltas = rest[4:9]
    normed, buffer = rest[9:]

    @pl.when(pl.program_id(0) == 0)
    def _():
        total = x[...].astype(F32) + load_sum(parts) + vec[BASELINE : BASELINE + 1]
        total = jnp.where(row_mask(total.shape), total, 0.0)
        resid[...] = total
        standard, _r = standardize(total)
        value = standard * vec[DILATION : DILATION + 1] + vec[ELEVATION : ELEVATION + 1]
        normed[...] = value.astype(BF16)
        normed_t[...] = value.T.astype(BF16)

    expanded = thresholds[...] + mm(normed[...], joined(weights, buffer))
    gate = jax.nn.sigmoid(SIGMOID_SLOPE * expanded)
    active = (expanded * gate).astype(BF16)
    hidden[...] = active
    slope[...] = (gate + SIGMOID_SLOPE * expanded * gate * (1.0 - gate)).astype(BF16)
    split_rows(mm(cot_t[...], active), deltas)


def forward_call(x, parts, vec, blocks, thresholds, cot_t):
    width = thresholds.shape[1]
    tile = min(512, width)
    cols = pl.BlockSpec((PAD, tile), lambda t: (0, t))
    return call(
        forward_kernel,
        (width // tile,),
        [whole((PAD, D))]
        + piece_specs() * 2
        + [whole(vec.shape)]
        + weight_specs(tile, lambda t: t)
        + [pl.BlockSpec((1, tile), lambda t: (0, t)), whole((D, PAD))],
        [whole((PAD, D)), whole((D, PAD)), cols, cols] + delta_specs(tile, lambda t: (0, t)),
        [sds((PAD, D), F32), sds((D, PAD)), sds((PAD, width)), sds((PAD, width))] + delta_shapes(width),
        4 * PAD * D * width,
        4 * D * width + 14 * PAD * D + 4 * PAD * width,
        [pltpu.VMEM((PAD, D), BF16), weight_buffer(tile)],
        transcendentals=PAD * width,
    )(x, *parts, vec, *blocks, thresholds, cot_t)


def backward_kernel(cot, *rest):
    narrow, (slope, hidden, normed_t), wide, rest = rest[:5], rest[5:8], rest[8:17], rest[17:]
    part, out, thresholds_sum = rest[:2], rest[2:4], rest[4]
    deltas, (total, out_total, buffer) = rest[5:10], rest[10:]
    step = pl.program_id(0)
    n = jnp.concatenate([n[...] for n in narrow], axis=0)
    grad = (mm(cot[...], n) * slope[...].astype(F32)).astype(BF16)
    out_term = mm_nt(hidden[...], n)
    thresholds_sum[...] = jnp.sum(grad.astype(F32), axis=0, keepdims=True)
    split_rows(mm(normed_t[...], grad), deltas)
    term = mm_nt(grad, joined(wide, buffer))

    @pl.when(step == 0)
    def _():
        total[...] = term
        out_total[...] = out_term

    @pl.when(step > 0)
    def _():
        total[...] += term
        out_total[...] += out_term

    @pl.when(step == pl.num_programs(0) - 1)
    def _():
        store_pieces(part, total[...])
        store_pieces(out, out_total[...])


def backward_call(cot, narrow_blocks, slope, hidden, normed_t, wide_blocks):
    width = slope.shape[1]
    tile = min(512, width)
    cols = pl.BlockSpec((PAD, tile), lambda t: (0, t))
    return call(
        backward_kernel,
        (width // tile,),
        [whole((PAD, D))]
        + plain_specs(tile, lambda t: t)
        + [cols, cols, whole((D, PAD))]
        + weight_specs(tile, lambda t: t),
        piece_specs() * 2 + [pl.BlockSpec((1, tile), lambda t: (0, t))] + delta_specs(tile, lambda t: (0, t)),
        piece_shapes() * 2 + [sds((1, width), F32)] + delta_shapes(width),
        8 * PAD * D * width,
        6 * D * width + 8 * PAD * D + 4 * PAD * width,
        [pltpu.VMEM((PAD, D), F32)] * 2 + [weight_buffer(tile)],
    )(cot, *narrow_blocks, slope, hidden, normed_t, *wide_blocks)


def resid_kernel(*rest):
    parts, (resid, cot, vec), rest = rest[:4], rest[4:7], rest[7:]
    weights, (grad_resid, grad_mixed, grad_t, sums, buffer) = rest[:9], rest[9:]
    upstream = load_sum(parts)
    standard, reciprocal = standardize(resid[...])
    sums[0:1] = jnp.sum(upstream * standard, axis=0, keepdims=True)
    sums[1:2] = jnp.sum(upstream, axis=0, keepdims=True)
    grad = cot[...].astype(F32) + norm_backward(upstream, standard, reciprocal, vec[DILATION : DILATION + 1])
    sums[2:3] = jnp.sum(grad, axis=0, keepdims=True)
    sums[3:4] = jnp.sum(cot[...].astype(F32), axis=0, keepdims=True)
    sums[4:8] = jnp.zeros((4, D), F32)
    grad_resid[...] = grad
    rounded = grad.astype(BF16)
    grad_mixed[...] = mm(rounded, joined(weights, buffer)).astype(BF16)
    grad_t[...] = grad.T.astype(BF16)


def resid_call(parts, resid, cot, vec, blocks):
    width = blocks[1].shape[1] // 4
    return call(
        resid_kernel,
        (1,),
        piece_specs() * 2 + [whole((PAD, D))] * 2 + [whole(vec.shape)] + weight_specs(width, lambda i: 3),
        [whole((PAD, D)), whole((PAD, width)), whole((D, PAD)), whole((8, D))],
        [sds((PAD, D), F32), sds((PAD, width)), sds((D, PAD)), sds((8, D), F32)],
        2 * PAD * D * width,
        16 * PAD * D + 2 * width * D + 2 * PAD * width,
        [weight_buffer(width)],
    )(*parts, resid, cot, vec, *blocks)


def attend_back_kernel(q, k, v, upstream, probs, grad_q, grad_k, grad_v):
    scaled = (q[...].astype(F32) * HD ** (-0.5)).astype(BF16)
    keys_t = (k[...].astype(F32) * HD ** (-0.5)).T.astype(BF16)
    values = v[...]
    up = upstream[...]
    grads_q = []
    kept_k = None
    kept_v = None
    for i in range(2):
        mask = head_mask(i, values.shape)
        rounded = probs[i]
        weights = rounded.astype(F32)
        picked = jnp.where(mask, values.astype(F32), 0.0).astype(BF16)
        weight_grad = mm_nt(picked, up)
        along = jnp.sum(weights * weight_grad, axis=0, keepdims=True)
        score_grad = (weights * (weight_grad - along)).astype(BF16)
        value_grad = mm(rounded, up)
        key_grad = mm(score_grad, scaled)
        kept_v = value_grad if i == 0 else jnp.where(mask, value_grad, kept_v)
        kept_k = key_grad if i == 0 else jnp.where(mask, key_grad, kept_k)
        grads_q.append(mm(keys_t[i * HD : (i + 1) * HD], score_grad))
    grad_q[...] = jnp.concatenate(grads_q, axis=0).T.astype(BF16)
    grad_k[...] = kept_k.astype(BF16)
    grad_v[...] = kept_v.astype(BF16)


def attend_back_call(qkv, upstream, probs):
    width = qkv.shape[1] // 3
    pairs = width // 128
    spec = lambda j: pl.BlockSpec((PAD, 128), lambda h, j=j: (0, j * pairs + h))
    return call(
        attend_back_kernel,
        (pairs,),
        [spec(0), spec(1), spec(2), spec(0), pl.BlockSpec((2, PAD, PAD), lambda h: (h, 0, 0))],
        [spec(0)] * 3,
        [sds((PAD, width))] * 3,
        pairs * 2 * 4 * 2 * PAD * PAD * 128,
        pairs * 2 * PAD * PAD * 2,
    )(qkv, qkv, qkv, upstream, probs)


def project_kernel(gq, gk, gv, normed_t, grad_t, mixed, *rest):
    weights, part, sums, deltas, (total, buffer) = rest[:9], rest[9:11], rest[11], rest[12:17], rest[17:]
    step = pl.program_id(0)

    def one(j, g):
        grad = g[...]
        sums[0] = jnp.sum(grad.astype(F32), axis=0, keepdims=True)
        split_rows(mm(normed_t[...], grad), deltas)
        term = mm_nt(grad, joined(weights, buffer))
        if j == 0:
            total[...] = term
        else:
            total[...] += term
        if j == 2:
            store_pieces(part, total[...])

    for j, g in enumerate((gq, gk, gv)):
        pl.when(step == j)(lambda j=j, g=g: one(j, g))

    @pl.when(step == 3)
    def _():
        split_rows(mm(grad_t[...], mixed[...]), deltas)


def project_call(grads, normed_t, grad_t, mixed, blocks):
    width = grads[0].shape[1]
    at = lambda j: jnp.minimum(j, 2)
    return call(
        project_kernel,
        (4,),
        [whole((PAD, width))] * 3 + [whole((D, PAD))] * 2 + [whole((PAD, width))] + weight_specs(width, at),
        piece_specs()
        + [pl.BlockSpec((1, 1, width), lambda j: (at(j), 0, 0))]
        + delta_specs(width, lambda j: (0, j)),
        piece_shapes() + [sds((3, 1, width), F32)] + delta_shapes(4 * width),
        4 * PAD * D * 3 * width + 2 * PAD * D * width,
        4 * D * 4 * width + 6 * PAD * D + 6 * PAD * width,
        [pltpu.VMEM((PAD, D), F32), weight_buffer(width)],
    )(*grads, normed_t, grad_t, mixed, *blocks)


def share(refs, at, value):
    owners, _rows, features = refs.shape
    for i in range(owners):
        refs[i, at : at + PAD] = value[:, i * features : (i + 1) * features].astype(BF16)


def tokens_kernel(*refs):
    parts, ffn_parts, (x, resid, grad_resid, cot, vec, deltas, sums) = refs[:4], refs[4:8], refs[8:]
    upstream = load_sum(parts)
    tokens = x[...].astype(F32)
    standard, reciprocal = standardize(tokens)
    sums[0:1] = jnp.sum(upstream * standard, axis=0, keepdims=True)
    sums[1:2] = jnp.sum(upstream, axis=0, keepdims=True)
    sums[2:8] = jnp.zeros((6, D), F32)
    share(deltas, 0, load_sum(ffn_parts) + vec[RESIDUE : RESIDUE + 1] + (resid[...] - tokens))
    grad = grad_resid[...] + norm_backward(upstream, standard, reciprocal, vec[STRETCH : STRETCH + 1])
    share(deltas, PAD, grad - cot[...].astype(F32))


def tokens_call(parts, ffn_parts, x, resid, grad_resid, cot, vec, features):
    return call(
        tokens_kernel,
        (1,),
        piece_specs() * 4 + [whole((PAD, D))] * 4 + [whole(vec.shape)],
        [whole((D // features, 2 * PAD, features)), whole((8, D))],
        [sds((D // features, 2 * PAD, features)), sds((8, D), F32)],
        24 * PAD * D,
        24 * PAD * D,
    )(*parts, *ffn_parts, x, resid, grad_resid, cot, vec)


def images_kernel(got, tokens, cot, layer, delta):
    for j in range(RB):
        at = slice(j * SEQ, (j + 1) * SEQ)
        layer[at] = got[j, :SEQ].astype(F32) + tokens[at].astype(F32)
        delta[at] = got[j, PAD : PAD + SEQ].astype(F32) + cot[at].astype(F32)


def images_call(got, tokens, cot):
    rows, features = tokens.shape
    return call(
        images_kernel,
        (1,),
        [whole(got.shape), whole((rows, features)), whole((rows, features))],
        [whole((rows, features))] * 2,
        [sds((rows, features), F32)] * 2,
        4 * rows * features,
        16 * rows * features,
    )(got, tokens, cot)


def swap(value, k):
    return lax.ppermute(value, "row", [(i, i ^ k) for i in range(RB)])


def after(value, *earlier):
    return lax.optimization_barrier((value,) + earlier)[0]


def sibling(part):
    size = lax.axis_size("col")
    if size == 2:
        return lax.ppermute(part, "col", [(0, 1), (1, 0)])
    total = None
    for s in range(1, size):
        term = lax.ppermute(part, "col", [(i, (i + s) % size) for i in range(size)]).astype(F32)
        total = term if total is None else total + term
    return total.astype(BF16)


def col_gather(values):
    size = lax.axis_size("col")
    lanes = values[0].shape[1]
    wide = jnp.concatenate(values, axis=1)
    if size == 2:
        other = lax.ppermute(wide, "col", [(0, 1), (1, 0)])
        first = lax.axis_index("col") == 0
        columns = [jnp.where(first, wide, other), jnp.where(first, other, wide)]
    else:
        columns = list(lax.all_gather(wide, "col"))
    parts = [column[:, k * lanes : (k + 1) * lanes] for k in range(len(values)) for column in columns]
    return jnp.concatenate(parts, axis=1)


class Gather:
    def __init__(self, clock, weight, *earlier):
        self.clock = clock
        self.plane = lax.axis_index("dp") % 2
        self.weight = weight
        shared = lax.dynamic_slice_in_dim(weight, PLANE + SHARED * self.plane, SHARED, axis=0)
        mine = after(jnp.concatenate([weight[:PLANE], shared]), *earlier)
        self.near = [swap(mine, 1), swap(mine, 2)]

    def across(self, value):
        return lax.ppermute(value, "dp", [(i, i ^ 1) for i in range(lax.axis_size("dp"))])

    def relay(self):
        near_x, near_y = self.near = self.clock(*self.near)
        self.far = [swap(near_x[:PLANE], 2), swap(near_y[PLANE:], 1)]
        self.other = [self.across(near_x[PLANE:]), self.across(near_y[PLANE:])]

    def hand_over(self, *earlier):
        *self.far, self.other[0] = self.clock(*self.far, self.other[0], *earlier)[:3]
        self.other.append(self.across(self.far[1]))

    def pieces(self):
        self.other[1:] = self.clock(*self.other[1:])
        return [self.plane.astype(jnp.int32)[None], self.weight, *self.near, *self.far, *self.other]


def add(*terms):
    total = terms[0].astype(F32)
    for term in terms[1:]:
        total = total + term.astype(F32)
    return total.astype(terms[0].dtype)


class Clock:
    def __init__(self):
        self.last = ()

    def __call__(self, *values):
        values = lax.optimization_barrier(tuple(values) + self.last)[: len(values)]
        self.last = values[:1]
        return values


class LineSum:
    def __init__(self, clock, value):
        size = lax.axis_size("dp")
        half = size // 2
        inward = [(s, s + 1) for s in range(half - 1)]
        self.clock = clock
        self.value = value
        if size % 2:
            self.value = lax.psum(value, "dp")
            self.steps = []
            return
        self.steps = [(None, [pair, (size - 1 - pair[0], size - 1 - pair[1])]) for pair in inward]
        self.steps.append((None, [(half - 1, half), (half, half - 1)]))
        for s, t in reversed(inward):
            self.steps.append((s, [(t, s), (size - 1 - t, size - 1 - s)]))
        self.send()

    def send(self):
        if self.steps:
            self.moved = lax.ppermute(self.value, "dp", self.steps[0][1])

    def advance(self):
        if not self.steps:
            return
        moved = self.clock(self.moved)[0]
        outer, pairs = self.steps.pop(0)
        if outer is None:
            self.value = add(self.value, moved)
        else:
            where = lax.axis_index("dp")
            far = lax.axis_size("dp") - 1 - outer
            self.value = jnp.where((where == outer) | (where == far), moved, self.value)
        self.send()


def first_sends(blocks):
    return swap(blocks[1], 1), swap(blocks[2], 2)


def last_terms(blocks, came):
    return add(blocks[3], came[1][: KB // 2]), add(blocks[4], came[0][: KB // 2])


def last_sends(terms):
    return swap(terms[0], 1), swap(terms[1], 2)


def own_sums(blocks, came, last):
    half = KB // 2
    return add(blocks[0][:half], came[0][half:], last[1]), add(blocks[0][half:], came[1][half:], last[0])


def afters(values, *earlier):
    return [after(value, *earlier) for value in values]


def per_device(
    tokens,
    projector,
    offsets,
    combiner,
    baseline,
    widener,
    thresholds,
    narrower,
    residue,
    stretch,
    lifting,
    dilation,
    elevation,
    cotangent,
):
    row = lax.axis_index("row")
    columns = lax.axis_size("col")
    features = tokens.shape[1]
    width = projector.shape[2]

    clock = Clock()

    def pick(stack, index, axis=0):
        return lax.dynamic_index_in_dim(stack, index, axis, keepdims=False)

    def padded(value):
        return jnp.pad(value.reshape(RB, SEQ, features), ((0, 0), (0, PAD - SEQ), (0, 0)))

    vectors = jnp.stack([stretch, lifting, baseline, dilation, elevation, residue, residue, residue])
    coarse = lax.optimization_barrier(vectors.astype(BF16))
    fine = (vectors - coarse.astype(F32)).astype(BF16)
    images = jnp.concatenate([padded(tokens), padded(cotangent)], axis=1)
    to = [jnp.concatenate([pick(images, row ^ k), coarse, fine]) for k in range(RB)]
    near = clock(*[swap(to[k], k) for k in range(1, RB)])
    attn_w = Gather(clock, jnp.concatenate([*projector, combiner.T], axis=1), *near)
    got = clock(col_gather([to[0], *near]))[0]
    x, cot = got[:PAD], got[PAD : 2 * PAD]
    vec = got[2 * PAD : 2 * PAD + 8].astype(F32) + got[2 * PAD + 8 :].astype(F32)
    x, cot, vec = clock(x, cot, vec)
    normed_one, normed_one_t, cot_t = clock(*norm_call(x, vec, cot))
    attn_w.relay()
    attn_w.hand_over()
    wide_w = Gather(clock, widener, *attn_w.far)
    attn_w = attn_w.pieces()
    wide_w.relay()

    bias = jnp.stack([offsets[0], jnp.zeros((width,), F32), offsets[1]])[:, None]
    qkv = qkv_call(normed_one, attn_w, bias)
    wide_w.hand_over(qkv)
    narrow = after(narrower.T, *wide_w.far)
    near_n = [swap(narrow, 1), swap(narrow, 2)]
    mixed, probs = attend_call(qkv)
    parts = combine_call(mixed, attn_w)
    others = [sibling(part) for part in parts]
    wide_w = wide_w.pieces()
    near_n = clock(*near_n)
    far_n = [swap(near_n[0][: KB // 2], 2), swap(near_n[1][KB // 2 :], 1)]
    others = clock(*others)
    out = forward_call(x, [*parts, *others], vec, wide_w, thresholds[None], cot_t)
    resid, normed_two_t, hidden, slope = out[:4]
    *far_n, slope = clock(*far_n, slope)
    blocks_n = afters(out[4:], *far_n)
    came_n = first_sends(blocks_n)
    narrow_w = [narrow, *near_n, *far_n]

    out = backward_call(cot, narrow_w, slope, hidden, normed_two_t, wide_w)
    parts, ffn_parts, thresholds_sum = out[:2], out[2:4], out[4]
    blocks_w = out[5:]
    *came_n, top = clock(*came_n, parts[0])
    parts = [top, parts[1]]
    terms = last_terms(blocks_n, came_n)
    last_n = last_sends(terms)
    came_w = list(first_sends(afters(blocks_w, *terms)))
    others = [sibling(part) for part in parts]
    grad_resid, grad_mixed, grad_t, sums_two = resid_call([*parts, *others], resid, cot, vec, attn_w)
    *last_n, grad_mixed = clock(*last_n, grad_mixed)
    halves = jnp.concatenate(own_sums(blocks_n, came_n, last_n))
    sum_n = LineSum(clock, halves)
    ffn_others = [sibling(after(part, *last_n)) for part in ffn_parts]
    grads = attend_back_call(qkv, after(grad_mixed, halves), probs)
    out = project_call(grads, normed_one_t, grad_t, mixed, attn_w)
    parts, grad_sums = out[:2], out[2]
    came_w[0], came_w[1], top, *ffn_others = clock(*came_w, parts[0], *ffn_others)
    parts = [top, parts[1]]
    terms = last_terms(blocks_w, came_w)
    last_w = list(last_sends(terms))
    blocks_p = afters(out[3:], *terms)
    came_p = list(first_sends(blocks_p))
    others = clock(*[sibling(part) for part in parts])
    deltas, sums_one = tokens_call(
        [*parts, *others], [*ffn_parts, *ffn_others], x, resid, grad_resid, cot, vec, features
    )
    featured = jnp.concatenate([sums_one[:2], sums_two[:4]]).reshape(6, RB, columns, features)
    featured = pick(featured, lax.axis_index("col"), 2)
    shared = jnp.concatenate([grad_sums[0, 0], grad_sums[2, 0], thresholds_sum[0]])
    size = 6 * features + shared.shape[0]
    lines = -(-size // (16 * features)) * 16
    mine = pick(deltas.reshape(RB, columns, 2 * PAD, features), lax.axis_index("col"), 1)
    fill = jnp.zeros((lines * features - size,), F32)
    to = []
    for j in range(RB):
        small = pick(featured, row ^ j, 1).reshape(-1)
        small = jnp.concatenate([small, shared, fill]).reshape(lines, features)
        to.append(jnp.concatenate([pick(mine, row ^ j), small.astype(BF16)]))
    last_w[0], last_w[1], to = clock(*last_w, jnp.stack(to))
    sum_w = [LineSum(clock, half) for half in own_sums(blocks_w, came_w, last_w)]
    sum_n.advance()
    came_p = clock(*came_p)
    last_p = last_sends(last_terms(blocks_p, came_p))
    sum_n.advance()
    sum_w[0].advance()
    sum_w[1].advance()
    last_p = clock(*last_p)
    halves_p = own_sums(blocks_p, came_p, last_p)
    sum_p = [LineSum(clock, half) for half in halves_p]
    got = lax.all_to_all(after(to, *halves_p), "row", 0, 0)
    sum_w[0].advance()
    sum_n.advance()
    sum_w[1].advance()
    sum_p[0].advance()
    sum_p[0].advance()
    sum_p[1].advance()
    got = clock(got)[0]
    small = got[:, 2 * PAD :].astype(F32)
    sum_s = LineSum(clock, sum([small[j] for j in range(1, RB)], small[0]))
    narrower_delta = clock(sum_n.value.astype(F32).T)[0]
    sum_w[0].advance()
    sum_w[1].advance()
    sum_p[1].advance()
    sum_s.advance()
    layer_output, tokens_delta = images_call(got, tokens, cotangent)
    sum_s.advance()
    for line_sum in (sum_n, sum_s, *sum_w, *sum_p):
        while line_sum.steps:
            line_sum.advance()
    widener_delta = jnp.concatenate([line_sum.value for line_sum in sum_w]).astype(F32)
    small = sum_s.value.reshape(-1)[:size]
    total_p = jnp.concatenate([line_sum.value for line_sum in sum_p]).astype(F32)
    projector_delta = jnp.stack([total_p[:, j * width : (j + 1) * width] for j in range(3)])
    combiner_delta = total_p[:, 3 * width :].T

    count = 6 * features
    vector = small[:count].reshape(6, features)
    offsets_delta = small[count : count + 2 * width].reshape(2, width)
    thresholds_delta = small[count + 2 * width :]
    return (
        layer_output,
        tokens_delta,
        projector_delta,
        offsets_delta,
        combiner_delta,
        vector[4],
        widener_delta,
        thresholds_delta,
        narrower_delta,
        vector[5],
        vector[0],
        vector[1],
        vector[2],
        vector[3],
    )


def solution(mesh):
    features = P(("row", "col"))
    specs = {
        "tokens": P("dp", ("row", "col")),
        "projector": P(None, "row", "col"),
        "offsets": P(None, "col"),
        "combiner": P("col", "row"),
        "baseline": features,
        "widener": P("row", "col"),
        "thresholds": P("col"),
        "narrower": P("col", "row"),
        "residue": features,
        "stretch": features,
        "lifting": features,
        "dilation": features,
        "elevation": features,
    }
    weights = tuple(specs.values())
    return jax.shard_map(
        per_device,
        mesh=mesh,
        in_specs=weights + (specs["tokens"],),
        out_specs=(specs["tokens"], specs["tokens"]) + weights[1:],
        check_vma=False,
    )
```

profile of v0, /device:TPU:0, one launch (start us, length us, event | category | flops | bytes accessed | tf_op | source)
XLA Modules:
  0.0 339.5 jit_solution(11509798746409303157)
XLA Ops:
  3.6 3.0 collective-permute-start
  8.2 6.6 %collective-permute-done = bf16[1200,128]{1,0:T(8,128)(2,1)S(1)} collective-permute-done((bf16[1200,128]{1,0:T(8,128)(2,1)S(1)}, bf16[1200,128]{1,0:T(8,128)(2,1)S(1)}, u32[]{:S(2)}, u32[]{:S(2)}) %collective-permute-start) | collective-permute-done | bytes 307232 | tf_op jit(solution)/shard_map/ppermute | solution.py:518
  14.7 7.2 %collective-permute-done.1 = bf16[1200,128]{1,0:T(8,128)(2,1)S(1)} collective-permute-done((bf16[1200,128]{1,0:T(8,128)(2,1)S(1)}, bf16[1200,128]{1,0:T(8,128)(2,1)S(1)}, u32[]{:S(2)}, u32[]{:S(2)}) %collective-permute-start.1) | collective-permute-done | bytes 307232 | tf_op jit(solution)/shard_map/ppermute | solution.py:518
  32.6 4.7 %shard_map.245 = (bf16[592,1024]{1,0:T(8,128)(2,1)}, bf16[1024,592]{1,0:T(8,128)(2,1)}, bf16[1024,592]{1,0:T(8,128)(2,1)}) custom-call(bf16[592,1024]{1,0:T(8,128)(2,1)} %get-tuple-element.155.x.refs_8_, f32[8,1024]{1,0:T(8,128)} %convert_add_fusion.vec.rest_4_.rest_6_.refs_12_, bf16[592,1024]{1,0:T(8,128)(2,1)} %get-tuple-element.153.cot.rest_5_.refs_11_), custom_call_target="tpu_custom_call" | custom-call | flops 94720 | bytes 94720 | tf_op jit(solution)/shard_map/pallas_call | solution.py:115
  37.3 6.8 %collective-permute-done.4.rest_2_.rest_9_ = bf16[176,2048]{1,0:T(8,128)(2,1)S(1)} collective-permute-done((bf16[176,2048]{1,0:T(8,128)(2,1)}, bf16[176,2048]{1,0:T(8,128)(2,1)S(1)}, u32[]{:S(2)}, u32[]{:S(2)}) %collective-permute-start.4) | collective-permute-done | bytes 720928 | tf_op jit(solution)/shard_map/ppermute | solution.py:518
  49.2 5.6 %collective-permute-done.7.rest_5_.rest_12_ = bf16[80,2048]{1,0:T(8,128)(2,1)S(1)} collective-permute-done((bf16[80,2048]{1,0:T(8,128)(2,1)S(1)}, bf16[80,2048]{1,0:T(8,128)(2,1)S(1)}, u32[]{:S(2)}, u32[]{:S(2)}) %collective-permute-start.7) | collective-permute-done | bytes 327712 | tf_op jit(solution)/shard_map/ppermute | solution.py:518
  59.9 8.6 %collective-permute-done.11.rest_7_.rest_14_ = bf16[80,2048]{1,0:T(8,128)(2,1)S(1)} collective-permute-done((bf16[80,2048]{1,0:T(8,128)(2,1)S(1)}, bf16[80,2048]{1,0:T(8,128)(2,1)S(1)}, u32[]{:S(2)}, u32[]{:S(2)}) %collective-permute-start.11) | collective-permute-done | bytes 327712 | tf_op jit(solution)/shard_map/ppermute | solution.py:560
  68.5 3.9 %collective-permute-done.12.rest_8_.rest_15_ = bf16[80,2048]{1,0:T(8,128)(2,1)S(1)} collective-permute-done((bf16[80,2048]{1,0:T(8,128)(2,1)S(1)}, bf16[80,2048]{1,0:T(8,128)(2,1)S(1)}, u32[]{:S(2)}, u32[]{:S(2)}) %collective-permute-start.12) | collective-permute-done | bytes 327712 | tf_op jit(solution)/shard_map/ppermute | solution.py:560
  81.8 6.0 %shard_map.246.q.k.v = bf16[592,1536]{1,0:T(8,128)(2,1)} custom-call(bf16[592,1024]{1,0:T(8,128)(2,1)} %get-tuple-element.160.normed, s32[1]{0:T(128)} %bitcast.15.rest_0_.rest_5_.rest_8_.rest_7_, bf16[256,2048]{1,0:T(8,128)(2,1)} %copy-done, bf16[176,2048]{1,0:T(8,128)(2,1)} %copy-done.1, bf16[176,2048]{1,0:T(8,128)(2,1)} %copy-done.2, ...), custom_call_target="tpu_custom_call" | custom-call | flops 29097984 | bytes 96512 | tf_op jit(solution)/shard_map/pallas_call | solution.py:165
  92.9 9.2 %shard_map.247 = (bf16[592,512]{1,0:T(8,128)(2,1)}, bf16[8,592,592]{2,1,0:T(8,128)(2,1)}) custom-call(bf16[592,1536]{1,0:T(8,128)(2,1)} %shard_map.246.q.k.v, bf16[592,1536]{1,0:T(8,128)(2,1)} %shard_map.246.q.k.v, bf16[592,1536]{1,0:T(8,128)(2,1)} %shard_map.246.q.k.v), custom_call_target="tpu_custom_call" | custom-call | flops 22429696 | bytes 87616 | tf_op jit(solution)/shard_map/pallas_call | solution.py:206
  102.1 3.3 shard_map.248
  105.9 4.4 %collective-permute-done.16.rest_1_ = bf16[256,2048]{1,0:T(8,128)(2,1)S(1)} collective-permute-done((bf16[256,2048]{1,0:T(8,128)(2,1)S(1)}, bf16[256,2048]{1,0:T(8,128)(2,1)S(1)}, u32[]{:S(2)}, u32[]{:S(2)}) %collective-permute-start.16) | collective-permute-done | bytes 1048608 | tf_op jit(solution)/shard_map/ppermute | solution.py:518
  116.2 15.0 %shard_map.249 = (f32[592,1024]{1,0:T(8,128)}, bf16[1024,592]{1,0:T(8,128)(2,1)}, bf16[592,2048]{1,0:T(8,128)(2,1)}, bf16[592,2048]{1,0:T(8,128)(2,1)}, bf16[256...) custom-call(bf16[592,1024]{1,0:T(8,128)(2,1)} %get-tuple-element.155, ...), custom_call_target="tpu_custom_call" | custom-call | flops 77594624 | bytes 339456 | tf_op jit(solution)/shard_map/pallas_call | solution.py:289
  132.9 18.7 %shard_map.250 = (bf16[304,1024]{1,0:T(8,128)(2,1)}, bf16[288,1024]{1,0:T(8,128)(2,1)}, bf16[304,1024]{1,0:T(8,128)(2,1)}, bf16[288,1024]{1,0:T(8,128)(2,1)}, f3...) custom-call(bf16[592,1024]{1,0:T(8,128)(2,1)} %get-tuple-element.153, ...), custom_call_target="tpu_custom_call" | custom-call | flops 155189248 | bytes 348160 | tf_op jit(solution)/shard_map/pallas_call | solution.py:338
  161.7 7.5 %shard_map.251 = (f32[592,1024]{1,0:T(8,128)}, bf16[592,512]{1,0:T(8,128)(2,1)}, bf16[1024,592]{1,0:T(8,128)(2,1)}, f32[8,1024]{1,0:T(8,128)}) custom-call(bf16[304,1024]{1,0:T(8,128)(2,1)} %get-tuple-element.207.rest_0_, bf16[288,1024]{1,0:T(8,128)(2,1)} %get-tuple-element.208.rest_1_, bf16[304,1024]{1,0:T(8,128)(2,1)} %copy-done.30, ...), custom_call_target="tpu_custom_call" | custom-call | flops 9699328 | bytes 177408 | tf_op jit(solution)/shard_map/pallas_call | solution.py:372
  169.7 3.2 collective-permute-done.28
  178.6 11.5 %shard_map.252 = (bf16[592,512]{1,0:T(8,128)(2,1)}, bf16[592,512]{1,0:T(8,128)(2,1)}, bf16[592,512]{1,0:T(8,128)(2,1)}) custom-call(bf16[592,1536]{1,0:T(8,128)(2,1)} %shard_map.246.q.k.v, bf16[592,1536]{1,0:T(8,128)(2,1)} %shard_map.246.q.k.v, bf16[592,1536]{1,0:T(8,128)(2,1)} %shard_map.246.q.k.v, bf16[592,512]{1,0:T(8,128)(2,1)} %get-tuple-element.216.upstream, ...), custom_call_target="tpu_custom_call" | custom-call | flops 44859392 | bytes 87616 | tf_op jit(solution)/shard_map/pallas_call | solution.py:414
  190.2 10.7 %shard_map.253 = (bf16[304,1024]{1,0:T(8,128)(2,1)}, bf16[288,1024]{1,0:T(8,128)(2,1)}, f32[3,1,512]{2,1,0:T(1,128)}, bf16[256,2048]{1,0:T(8,128)(2,1)}, bf16[25...) custom-call(bf16[592,512]{1,0:T(8,128)(2,1)} %get-tuple-element.218.gq, ...), custom_call_target="tpu_custom_call" | custom-call | flops 67895296 | bytes 216320 | tf_op jit(solution)/shard_map/pallas_call | solution.py:452
  210.4 8.6 %shard_map.254 = (bf16[8,1184,128]{2,1,0:T(8,128)(2,1)}, f32[8,1024]{1,0:T(8,128)}) custom-call(bf16[304,1024]{1,0:T(8,128)(2,1)} %get-tuple-element.231.refs_0_, bf16[288,1024]{1,0:T(8,128)(2,1)} %get-tuple-element.232.refs_1_, bf16[304,1024]{1,0:T(8,128)(2,1)} %collective-permute-done.36.refs_2_, bf16[288,1024]{1,0:T(8,128)(2,1)} %collective-permute-done.37.refs_3_, ...), custom_call_target="tpu_custom_call" | custom-call | flops 227328 | bytes 227328 | tf_op jit(solution)/shard_map/pallas_call | solution.py:486
  230.2 5.1 %collective-permute-start.44 = (bf16[128,2048]{1,0:T(8,128)(2,1)S(1)}, bf16[128,2048]{1,0:T(8,128)(2,1)S(1)}, u32[]{:S(2)}, u32[]{:S(2)}) collective-permute-start(bf16[128,2048]{1,0:T(8,128)(2,1)S(1)} %get-tuple-element.332), channel_id=1, source_target_pairs={{0,8},{24,16},{1,9},{25,17},{2,10},{26,18},{3,11},{27,19},{4,12},{... | collective-permute-start | bytes 1572872 | tf_op jit(solution)/shard_map/ppermute | solution.py:612
  236.6 4.4 %collective-permute-done.39 = bf16[256,2048]{1,0:T(8,128)(2,1)} collective-permute-done((bf16[256,2048]{1,0:T(8,128)(2,1)}, bf16[256,2048]{1,0:T(8,128)(2,1)}, u32[]{:S(2)}, u32[]{:S(2)}) %collective-permute-start.39) | collective-permute-done | bytes 1048608 | tf_op jit(solution)/shard_map/ppermute | solution.py:518
  250.9 5.6 %collective-permute-done.43 = bf16[128,2048]{1,0:T(8,128)(2,1)S(1)} collective-permute-done((bf16[128,2048]{1,0:T(8,128)(2,1)S(1)}, bf16[128,2048]{1,0:T(8,128)(2,1)S(1)}, u32[]{:S(2)}, u32[]{:S(2)}) %collective-permute-start.43) | collective-permute-done | bytes 524320 | tf_op jit(solution)/shard_map/ppermute | solution.py:612
  261.1 2.7 add_convert_fusion.10
  263.8 5.4 %collective-permute-start.47 = (bf16[128,2048]{1,0:T(8,128)(2,1)}, bf16[128,2048]{1,0:T(8,128)(2,1)}, u32[]{:S(2)}, u32[]{:S(2)}) collective-permute-start(bf16[128,2048]{1,0:T(8,128)(2,1)} %get-tuple-element.331), channel_id=1, source_target_pairs={{0,8},{24,16},{1,9},{25,17},{2,10},{26,18},{3,11},{27,19},{4,12},{... | collective-permute-start | bytes 1572872 | tf_op jit(solution)/shard_map/ppermute | solution.py:612
  271.3 3.5 %all-to-all-start = ((bf16[4,1216,128]{2,1,0:T(8,128)(2,1)}), bf16[4,1216,128]{2,1,0:T(8,128)(2,1)S(1)}, u32[]{:S(2)}, u32[]{:S(2)}) async-start(bf16[4,1216,128]{2,1,0:T(8,128)(2,1)} %pad_maximum_fusion.1), calls=%async_computation | async-start | bytes 2490368 | tf_op jit(solution)/shard_map/all_to_all | solution.py:765
  278.2 5.5 %collective-permute-done.49 = bf16[256,2048]{1,0:T(8,128)(2,1)} collective-permute-done((bf16[256,2048]{1,0:T(8,128)(2,1)S(1)}, bf16[256,2048]{1,0:T(8,128)(2,1)}, u32[]{:S(2)}, u32[]{:S(2)}) %collective-permute-start.49) | collective-permute-done | bytes 1048608 | tf_op jit(solution)/shard_map/ppermute | solution.py:612
  293.3 2.6 add_convert_fusion.6
  297.8 6.0 %collective-permute-done.55 = bf16[128,2048]{1,0:T(8,128)(2,1)} collective-permute-done((bf16[128,2048]{1,0:T(8,128)(2,1)}, bf16[128,2048]{1,0:T(8,128)(2,1)}, u32[]{:S(2)}, u32[]{:S(2)}) %collective-permute-start.55) | collective-permute-done | bytes 524320 | tf_op jit(solution)/shard_map/ppermute | solution.py:612
  303.8 5.8 %collective-permute-start.53 = (f32[32,128]{1,0:T(8,128)S(1)}, f32[32,128]{1,0:T(8,128)S(1)}, u32[]{:S(2)}, u32[]{:S(2)}) collective-permute-start(f32[32,128]{1,0:T(8,128)S(1)} %fusion.3), channel_id=1, source_target_pairs={{0,8},{24,16},{1,9},{25,17},{2,10},{26,18},{3,11},{27,19},{4,12},{... | collective-permute-start | bytes 49160 | tf_op jit(solution)/shard_map/ppermute | solution.py:612
  315.1 3.3 shard_map.255
  323.0 6.9 %collective-permute-done.58 = f32[32,128]{1,0:T(8,128)S(1)} collective-permute-done((f32[32,128]{1,0:T(8,128)S(1)}, f32[32,128]{1,0:T(8,128)S(1)}, u32[]{:S(2)}, u32[]{:S(2)}) %collective-permute-start.58) | collective-permute-done | bytes 16416 | tf_op jit(solution)/shard_map/ppermute | solution.py:612
  332.8 3.8 %collective-permute-done.59 = bf16[128,2048]{1,0:T(8,128)(2,1)S(1)} collective-permute-done((bf16[128,2048]{1,0:T(8,128)(2,1)S(1)}, bf16[128,2048]{1,0:T(8,128)(2,1)S(1)}, u32[]{:S(2)}, u32[]{:S(2)}) %collective-permute-start.59) | collective-permute-done | bytes 524320 | tf_op jit(solution)/shard_map/ppermute | solution.py:612
  (317 shorter events, 132.4 us)
Async XLA Ops:
  6.6 15.3 %collective-permute-start.1 = (bf16[1200,128]{1,0:T(8,128)(2,1)S(1)}, bf16[1200,128]{1,0:T(8,128)(2,1)S(1)}, u32[]{:S(2)}, u32[]{:S(2)}) collective-permute-start(bf16[1200,128]{1,0:T(8,128)(2,1)S(1)} %get-tuple-element.352), channel_id=1, source_target_pairs={{0,4},{2,6},{4,0},{6,2},{1,5},{3,7},{5,1},{7,3},{8,12},{10,14},{12... | collective-permute-start | bytes 921608 | tf_op jit(solution)/shard_map/ppermute | solution.py:518
  25.3 18.8 %collective-permute-start.4 = (bf16[176,2048]{1,0:T(8,128)(2,1)}, bf16[176,2048]{1,0:T(8,128)(2,1)S(1)}, u32[]{:S(2)}, u32[]{:S(2)}) collective-permute-start(bf16[176,2048]{1,0:T(8,128)(2,1)} %pad_maximum_fusion.6), channel_id=1, source_target_pairs={{0,2},{2,0},{4,6},{6,4},{1,3},{3,1},{5,7},{7,5},{8,10},{10,8},{12,... | collective-permute-start | bytes 2162696 | tf_op jit(solution)/shard_map/ppermute | solution.py:518
  26.5 18.5 %collective-permute-start.5 = (bf16[176,2048]{1,0:T(8,128)(2,1)}, bf16[176,2048]{1,0:T(8,128)(2,1)S(1)}, u32[]{:S(2)}, u32[]{:S(2)}) collective-permute-start(bf16[176,2048]{1,0:T(8,128)(2,1)} %pad_maximum_fusion.6), channel_id=1, source_target_pairs={{0,4},{2,6},{4,0},{6,2},{1,5},{3,7},{5,1},{7,3},{8,12},{10,14},{12... | collective-permute-start | bytes 2162696 | tf_op jit(solution)/shard_map/ppermute | solution.py:518
  56.0 16.4 %collective-permute-start.10 = (bf16[176,2048]{1,0:T(8,128)(2,1)S(1)}, bf16[176,2048]{1,0:T(8,128)(2,1)S(1)}, u32[]{:S(2)}, u32[]{:S(2)}) collective-permute-start(bf16[176,2048]{1,0:T(8,128)(2,1)S(1)} %pad_maximum_fusion.5), channel_id=1, source_target_pairs={{0,4},{2,6},{4,0},{6,2},{1,5},{3,7},{5,1},{7,3},{8,12},{10,14},{12... | collective-permute-start | bytes 2162696 | tf_op jit(solution)/shard_map/ppermute | solution.py:518
  56.6 16.2 %collective-permute-start.9 = (bf16[176,2048]{1,0:T(8,128)(2,1)S(1)}, bf16[176,2048]{1,0:T(8,128)(2,1)S(1)}, u32[]{:S(2)}, u32[]{:S(2)}) collective-permute-start(bf16[176,2048]{1,0:T(8,128)(2,1)S(1)} %pad_maximum_fusion.5), channel_id=1, source_target_pairs={{0,2},{2,0},{4,6},{6,4},{1,3},{3,1},{5,7},{7,5},{8,10},{10,8},{12,... | collective-permute-start | bytes 2162696 | tf_op jit(solution)/shard_map/ppermute | solution.py:518
  88.7 21.6 %collective-permute-start.16 = (bf16[256,2048]{1,0:T(8,128)(2,1)S(1)}, bf16[256,2048]{1,0:T(8,128)(2,1)S(1)}, u32[]{:S(2)}, u32[]{:S(2)}) collective-permute-start(bf16[256,2048]{1,0:T(8,128)(2,1)S(1)} %bitcast.84), channel_id=1, source_target_pairs={{0,2},{2,0},{4,6},{6,4},{1,3},{3,1},{5,7},{7,5},{8,10},{10,8},{12,... | collective-permute-start | bytes 3145736 | tf_op jit(solution)/shard_map/ppermute | solution.py:518
  89.9 21.7 %collective-permute-start.17 = (bf16[256,2048]{1,0:T(8,128)(2,1)S(1)}, bf16[256,2048]{1,0:T(8,128)(2,1)S(1)}, u32[]{:S(2)}, u32[]{:S(2)}) collective-permute-start(bf16[256,2048]{1,0:T(8,128)(2,1)S(1)} %bitcast.85), channel_id=1, source_target_pairs={{0,4},{2,6},{4,0},{6,2},{1,5},{3,7},{5,1},{7,3},{8,12},{10,14},{12... | collective-permute-start | bytes 3145736 | tf_op jit(solution)/shard_map/ppermute | solution.py:518
  112.4 18.8 %collective-permute-start.20 = (bf16[128,2048]{1,0:T(8,128)(2,1)}, bf16[128,2048]{1,0:T(8,128)(2,1)S(1)}, u32[]{:S(2)}, u32[]{:S(2)}) collective-permute-start(bf16[128,2048]{1,0:T(8,128)(2,1)} %slice.231), channel_id=1, source_target_pairs={{0,4},{2,6},{4,0},{6,2},{1,5},{3,7},{5,1},{7,3},{8,12},{10,14},{12... | collective-permute-start | bytes 1572872 | tf_op jit(solution)/shard_map/ppermute | solution.py:518
  114.8 16.5 %collective-permute-start.21 = (bf16[128,2048]{1,0:T(8,128)(2,1)}, bf16[128,2048]{1,0:T(8,128)(2,1)S(1)}, u32[]{:S(2)}, u32[]{:S(2)}) collective-permute-start(bf16[128,2048]{1,0:T(8,128)(2,1)} %slice.232), channel_id=1, source_target_pairs={{0,2},{2,0},{4,6},{6,4},{1,3},{3,1},{5,7},{7,5},{8,10},{10,8},{12,... | collective-permute-start | bytes 1572872 | tf_op jit(solution)/shard_map/ppermute | solution.py:518
  131.3 20.4 %collective-permute-start.25 = (bf16[256,2048]{1,0:T(8,128)(2,1)}, bf16[256,2048]{1,0:T(8,128)(2,1)S(1)}, u32[]{:S(2)}, u32[]{:S(2)}) collective-permute-start(bf16[256,2048]{1,0:T(8,128)(2,1)} %get-tuple-element.198), channel_id=1, source_target_pairs={{0,4},{2,6},{4,0},{6,2},{1,5},{3,7},{5,1},{7,3},{8,12},{10,14},{12... | collective-permute-start | bytes 3145736 | tf_op jit(solution)/shard_map/ppermute | solution.py:518
  132.2 19.5 %collective-permute-start.24 = (bf16[256,2048]{1,0:T(8,128)(2,1)}, bf16[256,2048]{1,0:T(8,128)(2,1)S(1)}, u32[]{:S(2)}, u32[]{:S(2)}) collective-permute-start(bf16[256,2048]{1,0:T(8,128)(2,1)} %get-tuple-element.196), channel_id=1, source_target_pairs={{0,2},{2,0},{4,6},{6,4},{1,3},{3,1},{5,7},{7,5},{8,10},{10,8},{12,... | collective-permute-start | bytes 3145736 | tf_op jit(solution)/shard_map/ppermute | solution.py:518
  159.2 42.3 %collective-permute-start.27 = (bf16[256,2048]{1,0:T(8,128)(2,1)}, bf16[256,2048]{1,0:T(8,128)(2,1)}, u32[]{:S(2)}, u32[]{:S(2)}) collective-permute-start(bf16[256,2048]{1,0:T(8,128)(2,1)} %get-tuple-element.206), channel_id=1, source_target_pairs={{0,4},{2,6},{4,0},{6,2},{1,5},{3,7},{5,1},{7,3},{8,12},{10,14},{12... | collective-permute-start | bytes 3145736 | tf_op jit(solution)/shard_map/ppermute | solution.py:518
  160.1 41.6 %collective-permute-start.26 = (bf16[256,2048]{1,0:T(8,128)(2,1)}, bf16[256,2048]{1,0:T(8,128)(2,1)}, u32[]{:S(2)}, u32[]{:S(2)}) collective-permute-start(bf16[256,2048]{1,0:T(8,128)(2,1)} %get-tuple-element.204), channel_id=1, source_target_pairs={{0,2},{2,0},{4,6},{6,4},{1,3},{3,1},{5,7},{7,5},{8,10},{10,8},{12,... | collective-permute-start | bytes 3145736 | tf_op jit(solution)/shard_map/ppermute | solution.py:518
  172.9 28.7 %collective-permute-start.33 = (bf16[288,1024]{1,0:T(8,128)(2,1)}, bf16[288,1024]{1,0:T(8,128)(2,1)}, u32[]{:S(2)}, u32[]{:S(2)}) collective-permute-start(bf16[288,1024]{1,0:T(8,128)(2,1)} %get-tuple-element.227.refs_5_), channel_id=1, source_target_pairs={{0,1},{1,0},{2,3},{3,2},{4,5},{5,4},{6,7},{7,6},{8,9},{9,8},{10,11... | collective-permute-start | bytes 1769480 | tf_op jit(solution)/shard_map/ppermute | solution.py:528
  172.9 28.7 %collective-permute-start.32 = (bf16[304,1024]{1,0:T(8,128)(2,1)}, bf16[304,1024]{1,0:T(8,128)(2,1)}, u32[]{:S(2)}, u32[]{:S(2)}) collective-permute-start(bf16[304,1024]{1,0:T(8,128)(2,1)} %get-tuple-element.225.refs_4_), channel_id=1, source_target_pairs={{0,1},{1,0},{2,3},{3,2},{4,5},{5,4},{6,7},{7,6},{8,9},{9,8},{10,11... | collective-permute-start | bytes 1867784 | tf_op jit(solution)/shard_map/ppermute | solution.py:528
  175.4 51.4 %collective-permute-start.40 = (bf16[256,2048]{1,0:T(8,128)(2,1)S(1)}, bf16[256,2048]{1,0:T(8,128)(2,1)S(1)}, u32[]{:S(2)}, u32[]{:S(2)}) collective-permute-start(bf16[256,2048]{1,0:T(8,128)(2,1)S(1)} %pad_maximum_fusion.4), channel_id=1, source_target_pairs={{0,8},{24,16},{1,9},{25,17},{2,10},{26,18},{3,11},{27,19},{4,12},{... | collective-permute-start | bytes 3145736 | tf_op jit(solution)/shard_map/ppermute | solution.py:612
  204.3 22.5 %collective-permute-start.35 = (bf16[128,2048]{1,0:T(8,128)(2,1)}, bf16[128,2048]{1,0:T(8,128)(2,1)}, u32[]{:S(2)}, u32[]{:S(2)}) collective-permute-start(bf16[128,2048]{1,0:T(8,128)(2,1)} %add_convert_fusion.16), channel_id=1, source_target_pairs={{0,4},{2,6},{4,0},{6,2},{1,5},{3,7},{5,1},{7,3},{8,12},{10,14},{12... | collective-permute-start | bytes 1572872 | tf_op jit(solution)/shard_map/ppermute | solution.py:518
  207.2 19.6 %collective-permute-start.34 = (bf16[128,2048]{1,0:T(8,128)(2,1)}, bf16[128,2048]{1,0:T(8,128)(2,1)}, u32[]{:S(2)}, u32[]{:S(2)}) collective-permute-start(bf16[128,2048]{1,0:T(8,128)(2,1)} %add_convert_fusion.17), channel_id=1, source_target_pairs={{0,2},{2,0},{4,6},{6,4},{1,3},{3,1},{5,7},{7,5},{8,10},{10,8},{12,... | collective-permute-start | bytes 1572872 | tf_op jit(solution)/shard_map/ppermute | solution.py:518
  208.6 32.4 %collective-permute-start.39 = (bf16[256,2048]{1,0:T(8,128)(2,1)}, bf16[256,2048]{1,0:T(8,128)(2,1)}, u32[]{:S(2)}, u32[]{:S(2)}) collective-permute-start(bf16[256,2048]{1,0:T(8,128)(2,1)} %get-tuple-element.249), channel_id=1, source_target_pairs={{0,4},{2,6},{4,0},{6,2},{1,5},{3,7},{5,1},{7,3},{8,12},{10,14},{12... | collective-permute-start | bytes 3145736 | tf_op jit(solution)/shard_map/ppermute | solution.py:518
  209.7 33.8 %collective-permute-start.38 = (bf16[256,2048]{1,0:T(8,128)(2,1)}, bf16[256,2048]{1,0:T(8,128)(2,1)}, u32[]{:S(2)}, u32[]{:S(2)}) collective-permute-start(bf16[256,2048]{1,0:T(8,128)(2,1)} %get-tuple-element.247), channel_id=1, source_target_pairs={{0,2},{2,0},{4,6},{6,4},{1,3},{3,1},{5,7},{7,5},{8,10},{10,8},{12,... | collective-permute-start | bytes 3145736 | tf_op jit(solution)/shard_map/ppermute | solution.py:518
  227.2 21.3 %collective-permute-start.45 = (bf16[256,2048]{1,0:T(8,128)(2,1)S(1)}, bf16[256,2048]{1,0:T(8,128)(2,1)S(1)}, u32[]{:S(2)}, u32[]{:S(2)}) collective-permute-start(bf16[256,2048]{1,0:T(8,128)(2,1)S(1)} %add_convert_fusion.1), channel_id=1, source_target_pairs={{8,16},{16,8},{9,17},{17,9},{10,18},{18,10},{11,19},{19,11},{12,20... | collective-permute-start | bytes 3145736 | tf_op jit(solution)/shard_map/ppermute | solution.py:612
  230.2 18.9 %collective-permute-start.44 = (bf16[128,2048]{1,0:T(8,128)(2,1)S(1)}, bf16[128,2048]{1,0:T(8,128)(2,1)S(1)}, u32[]{:S(2)}, u32[]{:S(2)}) collective-permute-start(bf16[128,2048]{1,0:T(8,128)(2,1)S(1)} %get-tuple-element.332), channel_id=1, source_target_pairs={{0,8},{24,16},{1,9},{25,17},{2,10},{26,18},{3,11},{27,19},{4,12},{... | collective-permute-start | bytes 1572872 | tf_op jit(solution)/shard_map/ppermute | solution.py:612
  235.3 21.2 %collective-permute-start.43 = (bf16[128,2048]{1,0:T(8,128)(2,1)S(1)}, bf16[128,2048]{1,0:T(8,128)(2,1)S(1)}, u32[]{:S(2)}, u32[]{:S(2)}) collective-permute-start(bf16[128,2048]{1,0:T(8,128)(2,1)S(1)} %get-tuple-element.333), channel_id=1, source_target_pairs={{0,8},{24,16},{1,9},{25,17},{2,10},{26,18},{3,11},{27,19},{4,12},{... | collective-permute-start | bytes 1572872 | tf_op jit(solution)/shard_map/ppermute | solution.py:612
  249.2 25.6 %collective-permute-start.50 = (bf16[128,2048]{1,0:T(8,128)(2,1)S(1)}, bf16[128,2048]{1,0:T(8,128)(2,1)}, u32[]{:S(2)}, u32[]{:S(2)}) collective-permute-start(bf16[128,2048]{1,0:T(8,128)(2,1)S(1)} %add_convert_fusion.8), channel_id=1, source_target_pairs={{8,16},{16,8},{9,17},{17,9},{10,18},{18,10},{11,19},{19,11},{12,20... | collective-permute-start | bytes 1572872 | tf_op jit(solution)/shard_map/ppermute | solution.py:612
  256.5 27.2 %collective-permute-start.49 = (bf16[256,2048]{1,0:T(8,128)(2,1)S(1)}, bf16[256,2048]{1,0:T(8,128)(2,1)}, u32[]{:S(2)}, u32[]{:S(2)}) collective-permute-start(bf16[256,2048]{1,0:T(8,128)(2,1)S(1)} %add_convert_fusion), channel_id=1, source_target_pairs={{8,0},{16,24},{9,1},{17,25},{10,2},{18,26},{11,3},{19,27},{12,4},{... | collective-permute-start | bytes 3145736 | tf_op jit(solution)/shard_map/ppermute | solution.py:612
  259.6 24.1 %collective-permute-start.48 = (bf16[128,2048]{1,0:T(8,128)(2,1)S(1)}, bf16[128,2048]{1,0:T(8,128)(2,1)}, u32[]{:S(2)}, u32[]{:S(2)}) collective-permute-start(bf16[128,2048]{1,0:T(8,128)(2,1)S(1)} %add_convert_fusion.9), channel_id=1, source_target_pairs={{8,16},{16,8},{9,17},{17,9},{10,18},{18,10},{11,19},{19,11},{12,20... | collective-permute-start | bytes 1572872 | tf_op jit(solution)/shard_map/ppermute | solution.py:612
  263.8 21.9 %collective-permute-start.47 = (bf16[128,2048]{1,0:T(8,128)(2,1)}, bf16[128,2048]{1,0:T(8,128)(2,1)}, u32[]{:S(2)}, u32[]{:S(2)}) collective-permute-start(bf16[128,2048]{1,0:T(8,128)(2,1)} %get-tuple-element.331), channel_id=1, source_target_pairs={{0,8},{24,16},{1,9},{25,17},{2,10},{26,18},{3,11},{27,19},{4,12},{... | collective-permute-start | bytes 1572872 | tf_op jit(solution)/shard_map/ppermute | solution.py:612
  269.2 21.2 %collective-permute-start.46 = (bf16[128,2048]{1,0:T(8,128)(2,1)}, bf16[128,2048]{1,0:T(8,128)(2,1)}, u32[]{:S(2)}, u32[]{:S(2)}) collective-permute-start(bf16[128,2048]{1,0:T(8,128)(2,1)} %get-tuple-element.330), channel_id=1, source_target_pairs={{0,8},{24,16},{1,9},{25,17},{2,10},{26,18},{3,11},{27,19},{4,12},{... | collective-permute-start | bytes 1572872 | tf_op jit(solution)/shard_map/ppermute | solution.py:612
  271.3 22.1 %all-to-all-start = ((bf16[4,1216,128]{2,1,0:T(8,128)(2,1)}), bf16[4,1216,128]{2,1,0:T(8,128)(2,1)S(1)}, u32[]{:S(2)}, u32[]{:S(2)}) async-start(bf16[4,1216,128]{2,1,0:T(8,128)(2,1)} %pad_maximum_fusion.1), calls=%async_computation | async-start | bytes 2490368 | tf_op jit(solution)/shard_map/all_to_all | solution.py:765
  276.9 19.1 %collective-permute-start.56 = (bf16[128,2048]{1,0:T(8,128)(2,1)}, bf16[128,2048]{1,0:T(8,128)(2,1)}, u32[]{:S(2)}, u32[]{:S(2)}) collective-permute-start(bf16[128,2048]{1,0:T(8,128)(2,1)} %add_convert_fusion.3), channel_id=1, source_target_pairs={{8,0},{16,24},{9,1},{17,25},{10,2},{18,26},{11,3},{19,27},{12,4},{... | collective-permute-start | bytes 1572872 | tf_op jit(solution)/shard_map/ppermute | solution.py:612
  287.7 16.1 %collective-permute-start.55 = (bf16[128,2048]{1,0:T(8,128)(2,1)}, bf16[128,2048]{1,0:T(8,128)(2,1)}, u32[]{:S(2)}, u32[]{:S(2)}) collective-permute-start(bf16[128,2048]{1,0:T(8,128)(2,1)} %add_convert_fusion.4), channel_id=1, source_target_pairs={{8,0},{16,24},{9,1},{17,25},{10,2},{18,26},{11,3},{19,27},{12,4},{... | collective-permute-start | bytes 1572872 | tf_op jit(solution)/shard_map/ppermute | solution.py:612
  310.7 20.9 %collective-permute-start.52 = (bf16[128,2048]{1,0:T(8,128)(2,1)}, bf16[128,2048]{1,0:T(8,128)(2,1)}, u32[]{:S(2)}, u32[]{:S(2)}) collective-permute-start(bf16[128,2048]{1,0:T(8,128)(2,1)} %add_convert_fusion.6), channel_id=1, source_target_pairs={{8,0},{16,24},{9,1},{17,25},{10,2},{18,26},{11,3},{19,27},{12,4},{... | collective-permute-start | bytes 1572872 | tf_op jit(solution)/shard_map/ppermute | solution.py:612
  (79 other events, 763.9 us)
where the time goes:
time: 346 us; the launch traced here: 339 us
  Pallas kernels  98.4 us (28%)
  waiting for transfers between devices  87.1 us (25%)
  starting transfers between devices  78.5 us (23%)
  other arithmetic  43 us (12%)
  local copies, waits for them, and re-layouts  30.6 us (9%)
    ppermute x27, waiting for transfers between devices, swap(): return lax.ppermute(value, 'row', [(i, i ^ k) for i in range(RB)])  45.4 us
    ppermute x18, starting transfers between devices, send(): self.moved = lax.ppermute(self.value, 'dp', self.steps[0][1])  35.7 us
    ppermute x27, starting transfers between devices, swap(): return lax.ppermute(value, 'row', [(i, i ^ k) for i in range(RB)])  29.8 us
    convert_element_type x19, other arithmetic, add(): return total.astype(terms[0].dtype)  28.4 us
    ppermute x18, waiting for transfers between devices, send(): self.moved = lax.ppermute(self.value, 'dp', self.steps[0][1])  27.9 us
    pallas_call x1, Pallas kernels, backward_call(): call(backward_kernel, (width // tile,), [whole((PAD, D))] + plain_specs(t...  18.7 us
    pallas_call x1, Pallas kernels, forward_call(): call(forward_kernel, (width // tile,), [whole((PAD, D))] + piece_specs()...  15 us
    unnamed x125, local copies, waits for them, and re-layouts  14.7 us
  transfers between devices with their start and end apart: 61, of which 21 were waited for; matrix products, arithmetic and copies ran while one was open for 18% of the time, Pallas kernels for 29%

commit v1 on v0

--- a/solution.py
+++ b/solution.py
@@ -775,9 +775,10 @@
     narrower_delta = clock(sum_n.value.astype(F32).T)[0]
     sum_w[0].advance()
     sum_w[1].advance()
+    sum_s.advance()
     sum_p[1].advance()
-    sum_s.advance()
-    layer_output, tokens_delta = images_call(got, tokens, cotangent)
+    layer_output, tokens_delta = images_call(after(got, sum_p[1].value), tokens, cotangent)
+    layer_output = clock(layer_output)[0]
     sum_s.advance()
     for line_sum in (sum_n, sum_s, *sum_w, *sum_p):
         while line_sum.steps:

time: 346 us -> 345 us (level)
    unnamed x125 -> x121, local copies, waits for them, and re-layouts: 14.7 us -> 13.9 us
where the time goes in v1:
time: 345 us; the launch traced here: 339 us
  Pallas kernels  98.5 us (29%)
  waiting for transfers between devices  89.5 us (26%)
  starting transfers between devices  75.2 us (22%)
  other arithmetic  43.8 us (13%)
  local copies, waits for them, and re-layouts  29.8 us (9%)
    ppermute x27, waiting for transfers between devices, swap(): return lax.ppermute(value, 'row', [(i, i ^ k) for i in range(RB)])  45.4 us
    ppermute x18, starting transfers between devices, send(): self.moved = lax.ppermute(self.value, 'dp', self.steps[0][1])  32.4 us
    ppermute x18, waiting for transfers between devices, send(): self.moved = lax.ppermute(self.value, 'dp', self.steps[0][1])  30.4 us
    ppermute x27, starting transfers between devices, swap(): return lax.ppermute(value, 'row', [(i, i ^ k) for i in range(RB)])  29.8 us
    convert_element_type x19, other arithmetic, add(): return total.astype(terms[0].dtype)  28.4 us
    pallas_call x1, Pallas kernels, backward_call(): call(backward_kernel, (width // tile,), [whole((PAD, D))] + plain_specs(t...  18.7 us
    pallas_call x1, Pallas kernels, forward_call(): call(forward_kernel, (width // tile,), [whole((PAD, D))] + piece_specs()...  15.1 us
    unnamed x121, local copies, waits for them, and re-layouts  13.9 us
  transfers between devices with their start and end apart: 61, of which 21 were waited for; matrix products, arithmetic and copies ran while one was open for 18% of the time, Pallas kernels for 29%

profile of v1, /device:TPU:0, one launch (start us, length us, event | category | flops | bytes accessed | tf_op | source)
XLA Modules:
  0.0 338.7 jit_solution(7246673030587382072)
XLA Ops:
  3.6 3.0 collective-permute-start
  8.2 6.6 %collective-permute-done = bf16[1200,128]{1,0:T(8,128)(2,1)S(1)} collective-permute-done((bf16[1200,128]{1,0:T(8,128)(2,1)S(1)}, bf16[1200,128]{1,0:T(8,128)(2,1)S(1)}, u32[]{:S(2)}, u32[]{:S(2)}) %collective-permute-start) | collective-permute-done | bytes 307232 | tf_op jit(solution)/shard_map/ppermute | solution.py:518
  14.7 7.2 %collective-permute-done.1 = bf16[1200,128]{1,0:T(8,128)(2,1)S(1)} collective-permute-done((bf16[1200,128]{1,0:T(8,128)(2,1)S(1)}, bf16[1200,128]{1,0:T(8,128)(2,1)S(1)}, u32[]{:S(2)}, u32[]{:S(2)}) %collective-permute-start.1) | collective-permute-done | bytes 307232 | tf_op jit(solution)/shard_map/ppermute | solution.py:518
  32.6 4.7 %shard_map.245 = (bf16[592,1024]{1,0:T(8,128)(2,1)}, bf16[1024,592]{1,0:T(8,128)(2,1)}, bf16[1024,592]{1,0:T(8,128)(2,1)}) custom-call(bf16[592,1024]{1,0:T(8,128)(2,1)} %get-tuple-element.157.x.refs_8_, f32[8,1024]{1,0:T(8,128)} %convert_add_fusion.vec.rest_4_.rest_6_.refs_12_, bf16[592,1024]{1,0:T(8,128)(2,1)} %get-tuple-element.155.cot.rest_5_.refs_11_), custom_call_target="tpu_custom_call" | custom-call | flops 94720 | bytes 94720 | tf_op jit(solution)/shard_map/pallas_call | solution.py:115
  37.2 6.8 %collective-permute-done.4.rest_2_.rest_9_ = bf16[176,2048]{1,0:T(8,128)(2,1)S(1)} collective-permute-done((bf16[176,2048]{1,0:T(8,128)(2,1)}, bf16[176,2048]{1,0:T(8,128)(2,1)S(1)}, u32[]{:S(2)}, u32[]{:S(2)}) %collective-permute-start.4) | collective-permute-done | bytes 720928 | tf_op jit(solution)/shard_map/ppermute | solution.py:518
  49.2 5.6 %collective-permute-done.7.rest_5_.rest_12_ = bf16[80,2048]{1,0:T(8,128)(2,1)S(1)} collective-permute-done((bf16[80,2048]{1,0:T(8,128)(2,1)S(1)}, bf16[80,2048]{1,0:T(8,128)(2,1)S(1)}, u32[]{:S(2)}, u32[]{:S(2)}) %collective-permute-start.7) | collective-permute-done | bytes 327712 | tf_op jit(solution)/shard_map/ppermute | solution.py:518
  59.9 8.6 %collective-permute-done.11.rest_7_.rest_14_ = bf16[80,2048]{1,0:T(8,128)(2,1)S(1)} collective-permute-done((bf16[80,2048]{1,0:T(8,128)(2,1)S(1)}, bf16[80,2048]{1,0:T(8,128)(2,1)S(1)}, u32[]{:S(2)}, u32[]{:S(2)}) %collective-permute-start.11) | collective-permute-done | bytes 327712 | tf_op jit(solution)/shard_map/ppermute | solution.py:560
  68.5 3.9 %collective-permute-done.12.rest_8_.rest_15_ = bf16[80,2048]{1,0:T(8,128)(2,1)S(1)} collective-permute-done((bf16[80,2048]{1,0:T(8,128)(2,1)S(1)}, bf16[80,2048]{1,0:T(8,128)(2,1)S(1)}, u32[]{:S(2)}, u32[]{:S(2)}) %collective-permute-start.12) | collective-permute-done | bytes 327712 | tf_op jit(solution)/shard_map/ppermute | solution.py:560
  81.8 6.0 %shard_map.246.q.k.v = bf16[592,1536]{1,0:T(8,128)(2,1)} custom-call(bf16[592,1024]{1,0:T(8,128)(2,1)} %get-tuple-element.162.normed, s32[1]{0:T(128)} %bitcast.15.rest_0_.rest_5_.rest_8_.rest_7_, bf16[256,2048]{1,0:T(8,128)(2,1)} %copy-done, bf16[176,2048]{1,0:T(8,128)(2,1)} %copy-done.1, bf16[176,2048]{1,0:T(8,128)(2,1)} %copy-done.2, ...), custom_call_target="tpu_custom_call" | custom-call | flops 29097984 | bytes 96512 | tf_op jit(solution)/shard_map/pallas_call | solution.py:165
  92.9 9.2 %shard_map.247 = (bf16[592,512]{1,0:T(8,128)(2,1)}, bf16[8,592,592]{2,1,0:T(8,128)(2,1)}) custom-call(bf16[592,1536]{1,0:T(8,128)(2,1)} %shard_map.246.q.k.v, bf16[592,1536]{1,0:T(8,128)(2,1)} %shard_map.246.q.k.v, bf16[592,1536]{1,0:T(8,128)(2,1)} %shard_map.246.q.k.v), custom_call_target="tpu_custom_call" | custom-call | flops 22429696 | bytes 87616 | tf_op jit(solution)/shard_map/pallas_call | solution.py:206
  102.1 3.3 shard_map.248
  105.9 4.4 %collective-permute-done.16.rest_1_ = bf16[256,2048]{1,0:T(8,128)(2,1)S(1)} collective-permute-done((bf16[256,2048]{1,0:T(8,128)(2,1)S(1)}, bf16[256,2048]{1,0:T(8,128)(2,1)S(1)}, u32[]{:S(2)}, u32[]{:S(2)}) %collective-permute-start.16) | collective-permute-done | bytes 1048608 | tf_op jit(solution)/shard_map/ppermute | solution.py:518
  116.2 15.1 %shard_map.249 = (f32[592,1024]{1,0:T(8,128)}, bf16[1024,592]{1,0:T(8,128)(2,1)}, bf16[592,2048]{1,0:T(8,128)(2,1)}, bf16[592,2048]{1,0:T(8,128)(2,1)}, bf16[256...) custom-call(bf16[592,1024]{1,0:T(8,128)(2,1)} %get-tuple-element.157, ...), custom_call_target="tpu_custom_call" | custom-call | flops 77594624 | bytes 339456 | tf_op jit(solution)/shard_map/pallas_call | solution.py:289
  132.9 18.7 %shard_map.250 = (bf16[304,1024]{1,0:T(8,128)(2,1)}, bf16[288,1024]{1,0:T(8,128)(2,1)}, bf16[304,1024]{1,0:T(8,128)(2,1)}, bf16[288,1024]{1,0:T(8,128)(2,1)}, f3...) custom-call(bf16[592,1024]{1,0:T(8,128)(2,1)} %get-tuple-element.155, ...), custom_call_target="tpu_custom_call" | custom-call | flops 155189248 | bytes 348160 | tf_op jit(solution)/shard_map/pallas_call | solution.py:338
  161.8 7.5 %shard_map.251 = (f32[592,1024]{1,0:T(8,128)}, bf16[592,512]{1,0:T(8,128)(2,1)}, bf16[1024,592]{1,0:T(8,128)(2,1)}, f32[8,1024]{1,0:T(8,128)}) custom-call(bf16[304,1024]{1,0:T(8,128)(2,1)} %get-tuple-element.209.rest_0_, bf16[288,1024]{1,0:T(8,128)(2,1)} %get-tuple-element.210.rest_1_, bf16[304,1024]{1,0:T(8,128)(2,1)} %copy-done.30, ...), custom_call_target="tpu_custom_call" | custom-call | flops 9699328 | bytes 177408 | tf_op jit(solution)/shard_map/pallas_call | solution.py:372
  169.8 3.2 collective-permute-done.28
  178.7 11.5 %shard_map.252 = (bf16[592,512]{1,0:T(8,128)(2,1)}, bf16[592,512]{1,0:T(8,128)(2,1)}, bf16[592,512]{1,0:T(8,128)(2,1)}) custom-call(bf16[592,1536]{1,0:T(8,128)(2,1)} %shard_map.246.q.k.v, bf16[592,1536]{1,0:T(8,128)(2,1)} %shard_map.246.q.k.v, bf16[592,1536]{1,0:T(8,128)(2,1)} %shard_map.246.q.k.v, bf16[592,512]{1,0:T(8,128)(2,1)} %get-tuple-element.218.upstream, ...), custom_call_target="tpu_custom_call" | custom-call | flops 44859392 | bytes 87616 | tf_op jit(solution)/shard_map/pallas_call | solution.py:414
  190.2 10.7 %shard_map.253 = (bf16[304,1024]{1,0:T(8,128)(2,1)}, bf16[288,1024]{1,0:T(8,128)(2,1)}, f32[3,1,512]{2,1,0:T(1,128)}, bf16[256,2048]{1,0:T(8,128)(2,1)}, bf16[25...) custom-call(bf16[592,512]{1,0:T(8,128)(2,1)} %get-tuple-element.220.gq, ...), custom_call_target="tpu_custom_call" | custom-call | flops 67895296 | bytes 216320 | tf_op jit(solution)/shard_map/pallas_call | solution.py:452
  210.4 8.6 %shard_map.254 = (bf16[8,1184,128]{2,1,0:T(8,128)(2,1)}, f32[8,1024]{1,0:T(8,128)}) custom-call(bf16[304,1024]{1,0:T(8,128)(2,1)} %get-tuple-element.233.refs_0_, bf16[288,1024]{1,0:T(8,128)(2,1)} %get-tuple-element.234.refs_1_, bf16[304,1024]{1,0:T(8,128)(2,1)} %collective-permute-done.36.refs_2_, bf16[288,1024]{1,0:T(8,128)(2,1)} %collective-permute-done.37.refs_3_, ...), custom_call_target="tpu_custom_call" | custom-call | flops 227328 | bytes 227328 | tf_op jit(solution)/shard_map/pallas_call | solution.py:486
  230.2 5.1 %collective-permute-start.44 = (bf16[128,2048]{1,0:T(8,128)(2,1)S(1)}, bf16[128,2048]{1,0:T(8,128)(2,1)S(1)}, u32[]{:S(2)}, u32[]{:S(2)}) collective-permute-start(bf16[128,2048]{1,0:T(8,128)(2,1)S(1)} %get-tuple-element.336), channel_id=1, source_target_pairs={{0,8},{24,16},{1,9},{25,17},{2,10},{26,18},{3,11},{27,19},{4,12},{... | collective-permute-start | bytes 1572872 | tf_op jit(solution)/shard_map/ppermute | solution.py:612
  236.6 4.4 %collective-permute-done.39 = bf16[256,2048]{1,0:T(8,128)(2,1)} collective-permute-done((bf16[256,2048]{1,0:T(8,128)(2,1)}, bf16[256,2048]{1,0:T(8,128)(2,1)}, u32[]{:S(2)}, u32[]{:S(2)}) %collective-permute-start.39) | collective-permute-done | bytes 1048608 | tf_op jit(solution)/shard_map/ppermute | solution.py:518
  241.0 2.6 collective-permute-done.38
  250.8 5.6 %collective-permute-done.43 = bf16[128,2048]{1,0:T(8,128)(2,1)S(1)} collective-permute-done((bf16[128,2048]{1,0:T(8,128)(2,1)S(1)}, bf16[128,2048]{1,0:T(8,128)(2,1)S(1)}, u32[]{:S(2)}, u32[]{:S(2)}) %collective-permute-start.43) | collective-permute-done | bytes 524320 | tf_op jit(solution)/shard_map/ppermute | solution.py:612
  261.1 2.7 add_convert_fusion.10
  263.8 5.4 %collective-permute-start.47 = (bf16[128,2048]{1,0:T(8,128)(2,1)}, bf16[128,2048]{1,0:T(8,128)(2,1)}, u32[]{:S(2)}, u32[]{:S(2)}) collective-permute-start(bf16[128,2048]{1,0:T(8,128)(2,1)} %get-tuple-element.335), channel_id=1, source_target_pairs={{0,8},{24,16},{1,9},{25,17},{2,10},{26,18},{3,11},{27,19},{4,12},{... | collective-permute-start | bytes 1572872 | tf_op jit(solution)/shard_map/ppermute | solution.py:612
  271.3 3.5 %all-to-all-start = ((bf16[4,1216,128]{2,1,0:T(8,128)(2,1)}), bf16[4,1216,128]{2,1,0:T(8,128)(2,1)S(1)}, u32[]{:S(2)}, u32[]{:S(2)}) async-start(bf16[4,1216,128]{2,1,0:T(8,128)(2,1)} %pad_maximum_fusion.1), calls=%async_computation | async-start | bytes 2490368 | tf_op jit(solution)/shard_map/all_to_all | solution.py:765
  278.2 5.5 %collective-permute-done.49 = bf16[256,2048]{1,0:T(8,128)(2,1)} collective-permute-done((bf16[256,2048]{1,0:T(8,128)(2,1)S(1)}, bf16[256,2048]{1,0:T(8,128)(2,1)}, u32[]{:S(2)}, u32[]{:S(2)}) %collective-permute-start.49) | collective-permute-done | bytes 1048608 | tf_op jit(solution)/shard_map/ppermute | solution.py:612
  293.3 2.6 add_convert_fusion.2
  297.1 6.8 %collective-permute-done.54 = bf16[128,2048]{1,0:T(8,128)(2,1)} collective-permute-done((bf16[128,2048]{1,0:T(8,128)(2,1)}, bf16[128,2048]{1,0:T(8,128)(2,1)}, u32[]{:S(2)}, u32[]{:S(2)}) %collective-permute-start.54) | collective-permute-done | bytes 524320 | tf_op jit(solution)/shard_map/ppermute | solution.py:612
  311.2 3.3 shard_map.255
  320.5 4.5 %collective-permute-done.58 = f32[32,128]{1,0:T(8,128)S(1)} collective-permute-done((f32[32,128]{1,0:T(8,128)S(1)}, f32[32,128]{1,0:T(8,128)S(1)}, u32[]{:S(2)}, u32[]{:S(2)}) %collective-permute-start.58) | collective-permute-done | bytes 16416 | tf_op jit(solution)/shard_map/ppermute | solution.py:612
  327.9 7.9 %collective-permute-done.59 = bf16[128,2048]{1,0:T(8,128)(2,1)S(1)} collective-permute-done((bf16[128,2048]{1,0:T(8,128)(2,1)S(1)}, bf16[128,2048]{1,0:T(8,128)(2,1)S(1)}, u32[]{:S(2)}, u32[]{:S(2)}) %collective-permute-start.59) | collective-permute-done | bytes 524320 | tf_op jit(solution)/shard_map/ppermute | solution.py:612
  (313 shorter events, 132.4 us)
Async XLA Ops:
  25.3 18.8 %collective-permute-start.4 = (bf16[176,2048]{1,0:T(8,128)(2,1)}, bf16[176,2048]{1,0:T(8,128)(2,1)S(1)}, u32[]{:S(2)}, u32[]{:S(2)}) collective-permute-start(bf16[176,2048]{1,0:T(8,128)(2,1)} %pad_maximum_fusion.6), channel_id=1, source_target_pairs={{0,2},{2,0},{4,6},{6,4},{1,3},{3,1},{5,7},{7,5},{8,10},{10,8},{12,... | collective-permute-start | bytes 2162696 | tf_op jit(solution)/shard_map/ppermute | solution.py:518
  26.5 18.5 %collective-permute-start.5 = (bf16[176,2048]{1,0:T(8,128)(2,1)}, bf16[176,2048]{1,0:T(8,128)(2,1)S(1)}, u32[]{:S(2)}, u32[]{:S(2)}) collective-permute-start(bf16[176,2048]{1,0:T(8,128)(2,1)} %pad_maximum_fusion.6), channel_id=1, source_target_pairs={{0,4},{2,6},{4,0},{6,2},{1,5},{3,7},{5,1},{7,3},{8,12},{10,14},{12... | collective-permute-start | bytes 2162696 | tf_op jit(solution)/shard_map/ppermute | solution.py:518
  56.0 16.4 %collective-permute-start.10 = (bf16[176,2048]{1,0:T(8,128)(2,1)S(1)}, bf16[176,2048]{1,0:T(8,128)(2,1)S(1)}, u32[]{:S(2)}, u32[]{:S(2)}) collective-permute-start(bf16[176,2048]{1,0:T(8,128)(2,1)S(1)} %pad_maximum_fusion.5), channel_id=1, source_target_pairs={{0,4},{2,6},{4,0},{6,2},{1,5},{3,7},{5,1},{7,3},{8,12},{10,14},{12... | collective-permute-start | bytes 2162696 | tf_op jit(solution)/shard_map/ppermute | solution.py:518
  56.6 16.2 %collective-permute-start.9 = (bf16[176,2048]{1,0:T(8,128)(2,1)S(1)}, bf16[176,2048]{1,0:T(8,128)(2,1)S(1)}, u32[]{:S(2)}, u32[]{:S(2)}) collective-permute-start(bf16[176,2048]{1,0:T(8,128)(2,1)S(1)} %pad_maximum_fusion.5), channel_id=1, source_target_pairs={{0,2},{2,0},{4,6},{6,4},{1,3},{3,1},{5,7},{7,5},{8,10},{10,8},{12,... | collective-permute-start | bytes 2162696 | tf_op jit(solution)/shard_map/ppermute | solution.py:518
  88.7 21.5 %collective-permute-start.16 = (bf16[256,2048]{1,0:T(8,128)(2,1)S(1)}, bf16[256,2048]{1,0:T(8,128)(2,1)S(1)}, u32[]{:S(2)}, u32[]{:S(2)}) collective-permute-start(bf16[256,2048]{1,0:T(8,128)(2,1)S(1)} %bitcast.84), channel_id=1, source_target_pairs={{0,2},{2,0},{4,6},{6,4},{1,3},{3,1},{5,7},{7,5},{8,10},{10,8},{12,... | collective-permute-start | bytes 3145736 | tf_op jit(solution)/shard_map/ppermute | solution.py:518
  89.9 21.6 %collective-permute-start.17 = (bf16[256,2048]{1,0:T(8,128)(2,1)S(1)}, bf16[256,2048]{1,0:T(8,128)(2,1)S(1)}, u32[]{:S(2)}, u32[]{:S(2)}) collective-permute-start(bf16[256,2048]{1,0:T(8,128)(2,1)S(1)} %bitcast.85), channel_id=1, source_target_pairs={{0,4},{2,6},{4,0},{6,2},{1,5},{3,7},{5,1},{7,3},{8,12},{10,14},{12... | collective-permute-start | bytes 3145736 | tf_op jit(solution)/shard_map/ppermute | solution.py:518
  112.4 18.9 %collective-permute-start.20 = (bf16[128,2048]{1,0:T(8,128)(2,1)}, bf16[128,2048]{1,0:T(8,128)(2,1)S(1)}, u32[]{:S(2)}, u32[]{:S(2)}) collective-permute-start(bf16[128,2048]{1,0:T(8,128)(2,1)} %slice.231), channel_id=1, source_target_pairs={{0,4},{2,6},{4,0},{6,2},{1,5},{3,7},{5,1},{7,3},{8,12},{10,14},{12... | collective-permute-start | bytes 1572872 | tf_op jit(solution)/shard_map/ppermute | solution.py:518
  114.8 16.5 %collective-permute-start.21 = (bf16[128,2048]{1,0:T(8,128)(2,1)}, bf16[128,2048]{1,0:T(8,128)(2,1)S(1)}, u32[]{:S(2)}, u32[]{:S(2)}) collective-permute-start(bf16[128,2048]{1,0:T(8,128)(2,1)} %slice.232), channel_id=1, source_target_pairs={{0,2},{2,0},{4,6},{6,4},{1,3},{3,1},{5,7},{7,5},{8,10},{10,8},{12,... | collective-permute-start | bytes 1572872 | tf_op jit(solution)/shard_map/ppermute | solution.py:518
  131.3 20.4 %collective-permute-start.25 = (bf16[256,2048]{1,0:T(8,128)(2,1)}, bf16[256,2048]{1,0:T(8,128)(2,1)S(1)}, u32[]{:S(2)}, u32[]{:S(2)}) collective-permute-start(bf16[256,2048]{1,0:T(8,128)(2,1)} %get-tuple-element.200), channel_id=1, source_target_pairs={{0,4},{2,6},{4,0},{6,2},{1,5},{3,7},{5,1},{7,3},{8,12},{10,14},{12... | collective-permute-start | bytes 3145736 | tf_op jit(solution)/shard_map/ppermute | solution.py:518
  132.3 19.5 %collective-permute-start.24 = (bf16[256,2048]{1,0:T(8,128)(2,1)}, bf16[256,2048]{1,0:T(8,128)(2,1)S(1)}, u32[]{:S(2)}, u32[]{:S(2)}) collective-permute-start(bf16[256,2048]{1,0:T(8,128)(2,1)} %get-tuple-element.198), channel_id=1, source_target_pairs={{0,2},{2,0},{4,6},{6,4},{1,3},{3,1},{5,7},{7,5},{8,10},{10,8},{12,... | collective-permute-start | bytes 3145736 | tf_op jit(solution)/shard_map/ppermute | solution.py:518
  159.2 42.3 %collective-permute-start.27 = (bf16[256,2048]{1,0:T(8,128)(2,1)}, bf16[256,2048]{1,0:T(8,128)(2,1)}, u32[]{:S(2)}, u32[]{:S(2)}) collective-permute-start(bf16[256,2048]{1,0:T(8,128)(2,1)} %get-tuple-element.208), channel_id=1, source_target_pairs={{0,4},{2,6},{4,0},{6,2},{1,5},{3,7},{5,1},{7,3},{8,12},{10,14},{12... | collective-permute-start | bytes 3145736 | tf_op jit(solution)/shard_map/ppermute | solution.py:518
  160.1 41.5 %collective-permute-start.26 = (bf16[256,2048]{1,0:T(8,128)(2,1)}, bf16[256,2048]{1,0:T(8,128)(2,1)}, u32[]{:S(2)}, u32[]{:S(2)}) collective-permute-start(bf16[256,2048]{1,0:T(8,128)(2,1)} %get-tuple-element.206), channel_id=1, source_target_pairs={{0,2},{2,0},{4,6},{6,4},{1,3},{3,1},{5,7},{7,5},{8,10},{10,8},{12,... | collective-permute-start | bytes 3145736 | tf_op jit(solution)/shard_map/ppermute | solution.py:518
  172.9 28.7 %collective-permute-start.33 = (bf16[288,1024]{1,0:T(8,128)(2,1)}, bf16[288,1024]{1,0:T(8,128)(2,1)}, u32[]{:S(2)}, u32[]{:S(2)}) collective-permute-start(bf16[288,1024]{1,0:T(8,128)(2,1)} %get-tuple-element.229.refs_5_), channel_id=1, source_target_pairs={{0,1},{1,0},{2,3},{3,2},{4,5},{5,4},{6,7},{7,6},{8,9},{9,8},{10,11... | collective-permute-start | bytes 1769480 | tf_op jit(solution)/shard_map/ppermute | solution.py:528
  172.9 28.7 %collective-permute-start.32 = (bf16[304,1024]{1,0:T(8,128)(2,1)}, bf16[304,1024]{1,0:T(8,128)(2,1)}, u32[]{:S(2)}, u32[]{:S(2)}) collective-permute-start(bf16[304,1024]{1,0:T(8,128)(2,1)} %get-tuple-element.227.refs_4_), channel_id=1, source_target_pairs={{0,1},{1,0},{2,3},{3,2},{4,5},{5,4},{6,7},{7,6},{8,9},{9,8},{10,11... | collective-permute-start | bytes 1867784 | tf_op jit(solution)/shard_map/ppermute | solution.py:528
  175.5 51.4 %collective-permute-start.40 = (bf16[256,2048]{1,0:T(8,128)(2,1)S(1)}, bf16[256,2048]{1,0:T(8,128)(2,1)S(1)}, u32[]{:S(2)}, u32[]{:S(2)}) collective-permute-start(bf16[256,2048]{1,0:T(8,128)(2,1)S(1)} %pad_maximum_fusion.4), channel_id=1, source_target_pairs={{0,8},{24,16},{1,9},{25,17},{2,10},{26,18},{3,11},{27,19},{4,12},{... | collective-permute-start | bytes 3145736 | tf_op jit(solution)/shard_map/ppermute | solution.py:612
  204.3 22.5 %collective-permute-start.35 = (bf16[128,2048]{1,0:T(8,128)(2,1)}, bf16[128,2048]{1,0:T(8,128)(2,1)}, u32[]{:S(2)}, u32[]{:S(2)}) collective-permute-start(bf16[128,2048]{1,0:T(8,128)(2,1)} %add_convert_fusion.16), channel_id=1, source_target_pairs={{0,4},{2,6},{4,0},{6,2},{1,5},{3,7},{5,1},{7,3},{8,12},{10,14},{12... | collective-permute-start | bytes 1572872 | tf_op jit(solution)/shard_map/ppermute | solution.py:518
  207.2 19.7 %collective-permute-start.34 = (bf16[128,2048]{1,0:T(8,128)(2,1)}, bf16[128,2048]{1,0:T(8,128)(2,1)}, u32[]{:S(2)}, u32[]{:S(2)}) collective-permute-start(bf16[128,2048]{1,0:T(8,128)(2,1)} %add_convert_fusion.17), channel_id=1, source_target_pairs={{0,2},{2,0},{4,6},{6,4},{1,3},{3,1},{5,7},{7,5},{8,10},{10,8},{12,... | collective-permute-start | bytes 1572872 | tf_op jit(solution)/shard_map/ppermute | solution.py:518
  208.6 32.4 %collective-permute-start.39 = (bf16[256,2048]{1,0:T(8,128)(2,1)}, bf16[256,2048]{1,0:T(8,128)(2,1)}, u32[]{:S(2)}, u32[]{:S(2)}) collective-permute-start(bf16[256,2048]{1,0:T(8,128)(2,1)} %get-tuple-element.251), channel_id=1, source_target_pairs={{0,4},{2,6},{4,0},{6,2},{1,5},{3,7},{5,1},{7,3},{8,12},{10,14},{12... | collective-permute-start | bytes 3145736 | tf_op jit(solution)/shard_map/ppermute | solution.py:518
  209.7 33.8 %collective-permute-start.38 = (bf16[256,2048]{1,0:T(8,128)(2,1)}, bf16[256,2048]{1,0:T(8,128)(2,1)}, u32[]{:S(2)}, u32[]{:S(2)}) collective-permute-start(bf16[256,2048]{1,0:T(8,128)(2,1)} %get-tuple-element.249), channel_id=1, source_target_pairs={{0,2},{2,0},{4,6},{6,4},{1,3},{3,1},{5,7},{7,5},{8,10},{10,8},{12,... | collective-permute-start | bytes 3145736 | tf_op jit(solution)/shard_map/ppermute | solution.py:518
  227.3 21.3 %collective-permute-start.45 = (bf16[256,2048]{1,0:T(8,128)(2,1)S(1)}, bf16[256,2048]{1,0:T(8,128)(2,1)S(1)}, u32[]{:S(2)}, u32[]{:S(2)}) collective-permute-start(bf16[256,2048]{1,0:T(8,128)(2,1)S(1)} %add_convert_fusion.1), channel_id=1, source_target_pairs={{8,16},{16,8},{9,17},{17,9},{10,18},{18,10},{11,19},{19,11},{12,20... | collective-permute-start | bytes 3145736 | tf_op jit(solution)/shard_map/ppermute | solution.py:612
  230.2 18.9 %collective-permute-start.44 = (bf16[128,2048]{1,0:T(8,128)(2,1)S(1)}, bf16[128,2048]{1,0:T(8,128)(2,1)S(1)}, u32[]{:S(2)}, u32[]{:S(2)}) collective-permute-start(bf16[128,2048]{1,0:T(8,128)(2,1)S(1)} %get-tuple-element.336), channel_id=1, source_target_pairs={{0,8},{24,16},{1,9},{25,17},{2,10},{26,18},{3,11},{27,19},{4,12},{... | collective-permute-start | bytes 1572872 | tf_op jit(solution)/shard_map/ppermute | solution.py:612
  235.3 21.2 %collective-permute-start.43 = (bf16[128,2048]{1,0:T(8,128)(2,1)S(1)}, bf16[128,2048]{1,0:T(8,128)(2,1)S(1)}, u32[]{:S(2)}, u32[]{:S(2)}) collective-permute-start(bf16[128,2048]{1,0:T(8,128)(2,1)S(1)} %get-tuple-element.337), channel_id=1, source_target_pairs={{0,8},{24,16},{1,9},{25,17},{2,10},{26,18},{3,11},{27,19},{4,12},{... | collective-permute-start | bytes 1572872 | tf_op jit(solution)/shard_map/ppermute | solution.py:612
  249.2 25.6 %collective-permute-start.50 = (bf16[128,2048]{1,0:T(8,128)(2,1)S(1)}, bf16[128,2048]{1,0:T(8,128)(2,1)}, u32[]{:S(2)}, u32[]{:S(2)}) collective-permute-start(bf16[128,2048]{1,0:T(8,128)(2,1)S(1)} %add_convert_fusion.8), channel_id=1, source_target_pairs={{8,16},{16,8},{9,17},{17,9},{10,18},{18,10},{11,19},{19,11},{12,20... | collective-permute-start | bytes 1572872 | tf_op jit(solution)/shard_map/ppermute | solution.py:612
  256.5 27.2 %collective-permute-start.49 = (bf16[256,2048]{1,0:T(8,128)(2,1)S(1)}, bf16[256,2048]{1,0:T(8,128)(2,1)}, u32[]{:S(2)}, u32[]{:S(2)}) collective-permute-start(bf16[256,2048]{1,0:T(8,128)(2,1)S(1)} %add_convert_fusion), channel_id=1, source_target_pairs={{8,0},{16,24},{9,1},{17,25},{10,2},{18,26},{11,3},{19,27},{12,4},{... | collective-permute-start | bytes 3145736 | tf_op jit(solution)/shard_map/ppermute | solution.py:612
  259.6 24.1 %collective-permute-start.48 = (bf16[128,2048]{1,0:T(8,128)(2,1)S(1)}, bf16[128,2048]{1,0:T(8,128)(2,1)}, u32[]{:S(2)}, u32[]{:S(2)}) collective-permute-start(bf16[128,2048]{1,0:T(8,128)(2,1)S(1)} %add_convert_fusion.9), channel_id=1, source_target_pairs={{8,16},{16,8},{9,17},{17,9},{10,18},{18,10},{11,19},{19,11},{12,20... | collective-permute-start | bytes 1572872 | tf_op jit(solution)/shard_map/ppermute | solution.py:612
  263.8 21.9 %collective-permute-start.47 = (bf16[128,2048]{1,0:T(8,128)(2,1)}, bf16[128,2048]{1,0:T(8,128)(2,1)}, u32[]{:S(2)}, u32[]{:S(2)}) collective-permute-start(bf16[128,2048]{1,0:T(8,128)(2,1)} %get-tuple-element.335), channel_id=1, source_target_pairs={{0,8},{24,16},{1,9},{25,17},{2,10},{26,18},{3,11},{27,19},{4,12},{... | collective-permute-start | bytes 1572872 | tf_op jit(solution)/shard_map/ppermute | solution.py:612
  269.2 21.2 %collective-permute-start.46 = (bf16[128,2048]{1,0:T(8,128)(2,1)}, bf16[128,2048]{1,0:T(8,128)(2,1)}, u32[]{:S(2)}, u32[]{:S(2)}) collective-permute-start(bf16[128,2048]{1,0:T(8,128)(2,1)} %get-tuple-element.334), channel_id=1, source_target_pairs={{0,8},{24,16},{1,9},{25,17},{2,10},{26,18},{3,11},{27,19},{4,12},{... | collective-permute-start | bytes 1572872 | tf_op jit(solution)/shard_map/ppermute | solution.py:612
  271.3 22.0 %all-to-all-start = ((bf16[4,1216,128]{2,1,0:T(8,128)(2,1)}), bf16[4,1216,128]{2,1,0:T(8,128)(2,1)S(1)}, u32[]{:S(2)}, u32[]{:S(2)}) async-start(bf16[4,1216,128]{2,1,0:T(8,128)(2,1)} %pad_maximum_fusion.1), calls=%async_computation | async-start | bytes 2490368 | tf_op jit(solution)/shard_map/all_to_all | solution.py:765
  276.9 19.0 %collective-permute-start.55 = (bf16[128,2048]{1,0:T(8,128)(2,1)}, bf16[128,2048]{1,0:T(8,128)(2,1)}, u32[]{:S(2)}, u32[]{:S(2)}) collective-permute-start(bf16[128,2048]{1,0:T(8,128)(2,1)} %add_convert_fusion.4), channel_id=1, source_target_pairs={{8,0},{16,24},{9,1},{17,25},{10,2},{18,26},{11,3},{19,27},{12,4},{... | collective-permute-start | bytes 1572872 | tf_op jit(solution)/shard_map/ppermute | solution.py:612
  287.7 16.1 %collective-permute-start.54 = (bf16[128,2048]{1,0:T(8,128)(2,1)}, bf16[128,2048]{1,0:T(8,128)(2,1)}, u32[]{:S(2)}, u32[]{:S(2)}) collective-permute-start(bf16[128,2048]{1,0:T(8,128)(2,1)} %add_convert_fusion.5), channel_id=1, source_target_pairs={{8,0},{16,24},{9,1},{17,25},{10,2},{18,26},{11,3},{19,27},{12,4},{... | collective-permute-start | bytes 1572872 | tf_op jit(solution)/shard_map/ppermute | solution.py:612
  308.9 17.9 %collective-permute-start.56 = (bf16[128,2048]{1,0:T(8,128)(2,1)}, bf16[128,2048]{1,0:T(8,128)(2,1)}, u32[]{:S(2)}, u32[]{:S(2)}) collective-permute-start(bf16[128,2048]{1,0:T(8,128)(2,1)} %add_convert_fusion.2), channel_id=1, source_target_pairs={{8,0},{16,24},{9,1},{17,25},{10,2},{18,26},{11,3},{19,27},{12,4},{... | collective-permute-start | bytes 1572872 | tf_op jit(solution)/shard_map/ppermute | solution.py:612
  319.2 16.6 %collective-permute-start.59 = (bf16[128,2048]{1,0:T(8,128)(2,1)S(1)}, bf16[128,2048]{1,0:T(8,128)(2,1)S(1)}, u32[]{:S(2)}, u32[]{:S(2)}) collective-permute-start(bf16[128,2048]{1,0:T(8,128)(2,1)S(1)} %add_convert_fusion.3), channel_id=1, source_target_pairs={{8,0},{16,24},{9,1},{17,25},{10,2},{18,26},{11,3},{19,27},{12,4},{... | collective-permute-start | bytes 1572872 | tf_op jit(solution)/shard_map/ppermute | solution.py:612
  (77 other events, 755.9 us)
